TPU v7x, 128 devices: a whole 4x4x4 slice. The times are simulated.
128 devices in a mesh: dp: 8 (over y, z_hi), fsdp: 16 (over z_lo, x, core).
Axes of the slice: x: 4, y: 4, z: 4 (z_hi: 2, z_lo: 2; z = z_hi * 2 + z_lo), core: 2. Of those that a mesh axis runs over, the one named last changes fastest.
Arguments:
- cap_hidden: bfloat16 [4096, 4096], P('dp'), may hold values from -6 to 6
- t5_norm_gain: bfloat16 [4096], replicated, may hold values from 0.5 to 1.5
- t5_wi0: bfloat16 [4096, 6144], P(None, 'fsdp'), may hold values from -0.09375 to 0.09375
- t5_wi1: bfloat16 [4096, 6144], P(None, 'fsdp'), may hold values from -0.09375 to 0.09375
- t5_wo: bfloat16 [6144, 4096], P('fsdp'), may hold values from -0.15625 to 0.15625
- t5_final_gain: bfloat16 [4096], replicated, may hold values from 0.5 to 1.5
- cap_lengths: int32 [16], P('dp'), may hold values from 1 to 256, 3072 in all
- latents: bfloat16 [16384, 4096], P(('dp', 'fsdp')), may hold values from -6 to 6
- w_query: bfloat16 [4096, 2048], P('fsdp'), may hold values from -0.109375 to 0.109375
- w_key: bfloat16 [4096, 2048], P(None, 'fsdp'), may hold values from -0.109375 to 0.109375
- w_value: bfloat16 [4096, 2048], P(None, 'fsdp'), may hold values from -0.09375 to 0.09375
- caption_of_image: int32 [16], P('dp'), may hold values from 0 to 1
- grad_out: bfloat16 [16384, 2048], P(('dp', 'fsdp')), may hold values from -6 to 6
Outputs:
- attn_out: float32 [16384, 2048], P(('dp', 'fsdp'))
- latent_token_gradient: float32 [16384, 4096], P(('dp', 'fsdp'))
- grad_query: float32 [4096, 2048], P('fsdp')
- grad_key: float32 [4096, 2048], P(None, 'fsdp')
- grad_value: float32 [4096, 2048], P(None, 'fsdp')
Inputs may be any that keep to these rules, and one draw needn't show every extreme that they name: `cap_lengths`: a caption's keys at positions at or past its length are masked; some caption has all 256 positions live. `caption_of_image`: an index among the 2 captions of the image's own dp index.
All inputs are finite; a program needn't handle non-finite values. No bound on the sum of `cap_lengths` on one device may be relied on, other than what follows from the above.
Results may differ from a plain program's by a relative error of at most 0.03.
Values may be sent and summed in bfloat16 or wider, within the bound.
A program may use at most 192 MiB of HBM per device.

v0:
```python
import math

import jax
import jax.numpy as jnp
from jax import lax
from jax.sharding import PartitionSpec as P

HD = 128
LCAP = 256
IMG_TOK = 1024


def rms_scale(values, gain):
    work = values.astype(jnp.float32)
    return (
        work
        * lax.rsqrt(jnp.mean(work * work, axis=-1, keepdims=True) + 1e-06)
        * gain.astype(jnp.float32)
    )


def attend(query_rows, grad_rows, key_rows, value_rows, lengths, owner):
    images = owner.shape[0]
    cap_count = lengths.shape[0]
    head_count = query_rows.shape[1] // HD
    inv_root = 1.0 / math.sqrt(HD)
    query_blocks = query_rows.reshape(images, IMG_TOK, head_count, HD)
    grad_blocks = grad_rows.reshape(images, IMG_TOK, head_count, HD)
    key_blocks = key_rows.reshape(cap_count, LCAP, head_count, HD)
    value_blocks = value_rows.reshape(cap_count, LCAP, head_count, HD)
    chosen = owner[:, None] == jnp.arange(cap_count, dtype=jnp.int32)[None, :]
    picker = chosen.astype(jnp.bfloat16)
    key_img = jnp.einsum(
        "ic,clhd->ilhd", picker, key_blocks, preferred_element_type=jnp.float32
    ).astype(jnp.bfloat16)
    value_img = jnp.einsum(
        "ic,clhd->ilhd", picker, value_blocks, preferred_element_type=jnp.float32
    ).astype(jnp.bfloat16)
    live_len = jnp.sum(jnp.where(chosen, lengths[None, :], 0), axis=1)
    live_mask = jnp.arange(LCAP, dtype=jnp.int32)[None, :] < live_len[:, None]
    scores = (
        jnp.einsum("ithd,ilhd->ihtl", query_blocks, key_img, preferred_element_type=jnp.float32)
        * inv_root
    )
    scores = jnp.where(live_mask[:, None, None, :], scores, -1e30)
    row_max = jnp.max(scores, axis=-1, keepdims=True)
    weights_exp = jnp.exp(scores - row_max)
    probs = weights_exp / jnp.sum(weights_exp, axis=-1, keepdims=True)
    probs_b = probs.astype(jnp.bfloat16)
    attn_blocks = jnp.einsum(
        "ihtl,ilhd->ithd", probs_b, value_img, preferred_element_type=jnp.float32
    )
    grad_probs = jnp.einsum(
        "ithd,ilhd->ihtl", grad_blocks, value_img, preferred_element_type=jnp.float32
    )
    grad_scores = (
        probs * (grad_probs - jnp.sum(probs * grad_probs, axis=-1, keepdims=True))
    ).astype(jnp.bfloat16)
    grad_queries = (
        jnp.einsum("ihtl,ilhd->ithd", grad_scores, key_img, preferred_element_type=jnp.float32)
        * inv_root
    ).astype(jnp.bfloat16)
    grad_key_img = (
        jnp.einsum("ihtl,ithd->ilhd", grad_scores, query_blocks, preferred_element_type=jnp.float32)
        * inv_root
    )
    grad_value_img = jnp.einsum(
        "ihtl,ithd->ilhd", probs_b, grad_blocks, preferred_element_type=jnp.float32
    )
    picker_f = chosen.astype(jnp.float32)
    grad_keys = jnp.einsum(
        "ic,ilhd->clhd", picker_f, grad_key_img, precision=lax.Precision.HIGHEST
    ).astype(jnp.bfloat16)
    grad_values = jnp.einsum(
        "ic,ilhd->clhd", picker_f, grad_value_img, precision=lax.Precision.HIGHEST
    ).astype(jnp.bfloat16)
    width = head_count * HD
    return (
        attn_blocks.reshape(images * IMG_TOK, width),
        grad_queries.reshape(images * IMG_TOK, width),
        grad_keys.reshape(cap_count * LCAP, width),
        grad_values.reshape(cap_count * LCAP, width),
    )


def local(
    cap_hidden,
    t5_norm_gain,
    t5_wi0,
    t5_wi1,
    t5_wo,
    t5_final_gain,
    cap_lengths,
    latents,
    w_query,
    w_key,
    w_value,
    caption_of_image,
    grad_out,
):
    normed = rms_scale(cap_hidden, t5_norm_gain).astype(jnp.bfloat16)
    gate_value = jnp.dot(normed, t5_wi0, preferred_element_type=jnp.float32)
    lift_value = jnp.dot(normed, t5_wi1, preferred_element_type=jnp.float32)
    hidden_act = (jax.nn.gelu(gate_value, approximate=True) * lift_value).astype(jnp.bfloat16)
    term_rows = jnp.dot(hidden_act, t5_wo, preferred_element_type=jnp.float32)
    ff_total = lax.psum(term_rows, "fsdp")
    caption = rms_scale(cap_hidden.astype(jnp.float32) + ff_total, t5_final_gain).astype(
        jnp.bfloat16
    )
    key_rows = jnp.dot(caption, w_key, preferred_element_type=jnp.float32).astype(jnp.bfloat16)
    value_rows = jnp.dot(caption, w_value, preferred_element_type=jnp.float32).astype(jnp.bfloat16)
    lat = latents.astype(jnp.float32)
    mean_removed_input = lat - jnp.mean(lat, axis=-1, keepdims=True)
    reciprocal_deviation = lax.rsqrt(
        jnp.mean(mean_removed_input * mean_removed_input, axis=-1, keepdims=True) + 1e-06
    )
    standardized_input = mean_removed_input * reciprocal_deviation
    normalized_latent_rows = standardized_input.astype(jnp.bfloat16)
    query_full = lax.all_gather(w_query, "fsdp", axis=0, tiled=True)
    query_tok = jnp.dot(
        normalized_latent_rows, query_full, preferred_element_type=jnp.float32
    ).astype(jnp.bfloat16)
    query_heads = lax.all_to_all(query_tok, "fsdp", split_axis=1, concat_axis=0, tiled=True)
    grad_heads = lax.all_to_all(grad_out, "fsdp", split_axis=1, concat_axis=0, tiled=True)
    attn_heads, grad_query_heads, grad_keys, grad_values = attend(
        query_heads, grad_heads, key_rows, value_rows, cap_lengths, caption_of_image
    )
    attn_out = lax.all_to_all(
        attn_heads.astype(jnp.bfloat16), "fsdp", split_axis=0, concat_axis=1, tiled=True
    ).astype(attn_heads.dtype)
    grad_query_tok = lax.all_to_all(
        grad_query_heads, "fsdp", split_axis=0, concat_axis=1, tiled=True
    )
    normalized_input_gradient = lax.dot_general(
        grad_query_tok, query_full, (((1,), (1,)), ((), ())), preferred_element_type=jnp.float32
    )
    query_grad_rows = lax.psum_scatter(
        lax.dot_general(
            normalized_latent_rows,
            grad_query_tok,
            (((0,), (0,)), ((), ())),
            preferred_element_type=jnp.float32,
        ).astype(jnp.bfloat16),
        "fsdp",
        scatter_dimension=0,
        tiled=True,
    )
    latent_token_gradient = reciprocal_deviation * (
        normalized_input_gradient
        - jnp.mean(normalized_input_gradient, axis=-1, keepdims=True)
        - standardized_input
        * jnp.mean(normalized_input_gradient * standardized_input, axis=-1, keepdims=True)
    )
    key_part = lax.dot_general(
        caption, grad_keys, (((0,), (0,)), ((), ())), preferred_element_type=jnp.float32
    )
    value_part = lax.dot_general(
        caption, grad_values, (((0,), (0,)), ((), ())), preferred_element_type=jnp.float32
    )
    grad_query, grad_key, grad_value = (
        lax.psum(query_grad_rows, "dp").astype(jnp.float32),
        lax.psum(key_part.astype(jnp.bfloat16), "dp").astype(jnp.float32),
        lax.psum(value_part.astype(jnp.bfloat16), "dp").astype(jnp.float32),
    )
    return (attn_out, latent_token_gradient, grad_query, grad_key, grad_value)


def solution(mesh):
    placed = (
        P("dp", None),
        P(),
        P(None, "fsdp"),
        P(None, "fsdp"),
        P("fsdp", None),
        P(),
        P("dp"),
        P(("dp", "fsdp"), None),
        P("fsdp", None),
        P(None, "fsdp"),
        P(None, "fsdp"),
        P("dp"),
        P(("dp", "fsdp"), None),
    )
    return jax.shard_map(
        local,
        mesh=mesh,
        in_specs=placed,
        out_specs=(
            P(("dp", "fsdp"), None),
            P(("dp", "fsdp"), None),
            P("fsdp", None),
            P(None, "fsdp"),
            P(None, "fsdp"),
        ),
        check_vma=False,
    )
```

profile of v0, /device:TPU:0, one launch (start us, length us, event | category | flops | bytes accessed | tf_op | source)
XLA Modules:
  0.0 596.4 jit_solution(5784977476985465292)
XLA Ops:
  7.2 0.9 convert_element_type.110
  8.1 3.4 fusion.1
  11.5 5.2 fusion.37
  16.8 11.0 %fusion.22 = f32[512,4096]{1,0:T(8,128)} fusion(bf16[384,4096]{1,0:T(8,128)(2,1)S(1)} %copy-done, f32[512,384]{1,0:T(8,128)} %fusion.37, bf16[4096,384]{1,0:T(8,128)(2,1)} %param.16, bf16[512,4096]{1,0:T(8,128)(2,1)} %param.13, f32[4096]{0:T(1024)S(1)} %convert_element_type.110, f32[512]{0:T(512)S(1)} %add_rsqrt_fusion.1), kind=kOutput, calls=%fused_computation.40 | convolution fusion | flops 3230007296 | bytes 19679232 | tf_op jit(solution)/shard_map/dot_general | solution.py:105
  28.1 0.5 all-gather.2.cloned.1.call-update
  28.7 0.3 copy-done.4
  29.3 0.4 fusion.12
  29.8 0.9 copy_bitcast_fusion
  30.8 142.5 %all-reduce.4.cloned.1.call-done = f32[512,4096]{1,0:T(8,128)} async-done(((f32[512,4096]{1,0:T(8,128)}), f32[512,4096]{1,0:T(8,128)}) %all-reduce.4.cloned.1.call-update) | async-done | bytes 8388624 | tf_op jit(solution)/shard_map/psum | solution.py:106
  173.3 5.9 multiply_reduce_fusion
  179.2 5.4 multiply_convert_fusion
  184.6 2.0 copy-done.2
  186.7 1.2 convolution_convert_fusion.8
  187.9 79.0 %all-gather.2.cloned.1.call-done = bf16[4096,2048]{1,0:T(8,128)(2,1)} async-done(((bf16[256,2048]{1,0:T(8,128)(2,1)}), bf16[4096,2048]{1,0:T(8,128)(2,1)}) %all-gather.2.cloned.1.call-update) | async-done | bytes 16777232 | tf_op jit(solution)/shard_map/all_gather | solution.py:119
  267.0 8.2 %fusion.19 = bf16[16,16,8,128]{3,2,1,0:T(8,128)(2,1)S(1)} fusion(bf16[4096,2048]{1,0:T(8,128)(2,1)} %all-gather.2.cloned.1.call-done, bf16[128,4096]{1,0:T(8,128)(2,1)S(1)} %copy-done.4, f32[128]{0:T(128)S(1)} %add_rsqrt_fusion.2, f32[128]{0:T(128)S(1)} %broadcast_multiply_fusion.2), kind=kOutput, calls=%fused_computation.37 | convolution fusion | flops 2149842944 | bytes 18351104 | tf_op jit(solution)/shard_map/dot_general | solution.py:120
  275.1 0.9 copy.123
  276.1 5.0 all-to-all-start
  281.0 0.3 convolution_convert_fusion.7
  281.5 3.4 convolution_convert_fusion.10
  285.0 6.9 %all-to-all-done = bf16[128,16,128]{2,0,1:T(8,128)(2,1)S(1)} async-done(((bf16[128,16,128]{2,0,1:T(8,128)(2,1)}), bf16[128,16,128]{2,0,1:T(8,128)(2,1)S(1)}, u32[]{:S(2)}, u32[]{:S(2)}) %all-to-all-start) | async-done | bytes 524320 | tf_op jit(solution)/shard_map/all_to_all | solution.py:123
  291.9 3.6 all-to-all-start.2
  295.5 0.3 convolution_convert_fusion.9
  295.9 2.2 fusion.64
  298.1 8.2 %all-to-all-done.2 = bf16[128,16,128]{2,0,1:T(8,128)(2,1)S(1)} async-done(((bf16[128,16,128]{2,0,1:T(8,128)(2,1)}), bf16[128,16,128]{2,0,1:T(8,128)(2,1)S(1)}, u32[]{:S(2)}, u32[]{:S(2)}) %all-to-all-start.2) | async-done | bytes 524320 | tf_op jit(solution)/shard_map/all_to_all | solution.py:124
  306.3 2.3 fusion.13
  308.7 0.5 fusion.15
  309.6 1.0 copy.90
  310.6 15.1 %all_to_all.61 = bf16[16,128,128]{2,1,0:T(8,128)(2,1)} all-to-all(bf16[16,128,128]{2,1,0:T(8,128)(2,1)} %bitcast.90), channel_id=1, replica_groups=mesh['dp'=8,'fsdp'=16] {'fsdp'}, dimensions={0} | all-to-all | bytes 1048576 | tf_op jit(solution)/shard_map/all_to_all | solution.py:131
  325.7 1.3 copy.91
  327.0 8.3 %convolution_convert_fusion = bf16[4096,2048]{1,0:T(8,128)(2,1)} fusion(bf16[128,2048]{0,1:T(8,128)(2,1)S(1)} %bitcast.85, bf16[128,4096]{1,0:T(8,128)(2,1)S(1)} %copy-done.4, f32[128]{0:T(128)S(1)} %add_rsqrt_fusion.2, f32[128]{0:T(128)S(1)} %broadcast_multiply_fusion.2), kind=kOutput, calls=%fused_computation.1 | convolution fusion | flops 2157969408 | bytes 18351104 | tf_op jit(solution)/shard_map/dot_general | solution.py:138
  335.4 0.5 fusion.27
  336.0 0.6 convolution_convert_fusion.6
  336.6 2.2 fusion.40
  338.9 0.7 convolution_convert_fusion.5
  339.6 2.3 convolution_convert_fusion.2
  341.9 2.3 convolution_convert_fusion.1
  344.2 88.1 %reduce-scatter.2.cloned.1.call-done = bf16[256,2048]{1,0:T(8,128)(2,1)} async-done(((bf16[4096,2048]{1,0:T(8,128)(2,1)}), bf16[256,2048]{1,0:T(8,128)(2,1)}) %reduce-scatter.2.cloned.1.call-update) | async-done | bytes 1048592 | tf_op jit(solution)/shard_map/reduce_scatter | solution.py:137
  432.4 1.1 fusion.21
  433.5 1.3 copy.84
  434.8 14.3 %all_to_all.62 = bf16[16,128,128]{2,1,0:T(8,128)(2,1)S(1)} all-to-all(bf16[16,128,128]{2,1,0:T(8,128)(2,1)S(1)} %bitcast.92), channel_id=1, replica_groups=mesh['dp'=8,'fsdp'=16] {'fsdp'}, dimensions={0} | all-to-all | bytes 1048576 | tf_op jit(solution)/shard_map/all_to_all | solution.py:128
  449.3 0.3 copy.85
  449.6 1.3 copy.98
  450.9 11.8 %fusion.63 = (f32[128]{0:T(128)S(1)}, f32[128]{0:T(128)S(1)}, f32[128,4096]{1,0:T(8,128)S(1)}) fusion(f32[128]{0:T(128)S(1)} %add_rsqrt_fusion.2, f32[128]{0:T(128)S(1)} %broadcast_multiply_fusion.2, bf16[128,4096]{1,0:T(8,128)(2,1)S(1)} %copy-done.4, bf16[128,2048]{0,1:T(8,128)(2,1)} %bitcast.86, bf16[4096,2048]{1,0:T(8,128)(2,1)} %all-gather.2.cloned.1.call-done), kind=kOutput, calls=%fused_computation.94 | convolution fusion | flops 2150629376 | bytes 20449280 | tf_op jit(solution)/shard_map/dot_general | solution.py:134
  462.8 2.0 fusion.11
  464.7 119.2 %all-reduce.6.cloned.1.call-done = (bf16[256,2048]{1,0:T(8,128)(2,1)}, bf16[4096,128]{1,0:T(8,128)(2,1)}, bf16[4096,128]{1,0:T(8,128)(2,1)}) async-done(((bf16[256,2048]{1,0:T(8,128)(2,1)}, bf16[4096,128]{1,0:T(8,128)(2,1)}, bf16[4096,128]{1,0:T(8,128)(2,1)}), (bf16[256,2048]{1,0:T(8,128)(2,1)}, bf16[4096,128]{1,0:T(8,128)(2,1)}, bf16[4096,128]{1,0:T(8,128)(2,1)})) %all-reduce.6.cloned.1.call-update) | async-done | bytes 3145744 | tf_op jit(solution)/shard_map/psum | solution.py:161
  584.0 2.9 convert_element_type.135
  586.9 1.5 convert_element_type.138
  588.4 1.5 convert_element_type.141
  (62 shorter events, 1.7 us)
Async XLA Ops:
  7.2 9.6 %copy-start = (bf16[384,4096]{1,0:T(8,128)(2,1)S(1)}, bf16[384,4096]{1,0:T(8,128)(2,1)}, u32[]{:S(2)}) copy-start(bf16[384,4096]{1,0:T(8,128)(2,1)} %param.17) | copy-start | bytes 9437188
  7.2 166.1 %all-reduce.4.cloned.1.call-start = ((), (), s32[]{:S(2)}) async-start(), calls=%async_computation.5 | async-start | bytes 16777216 | tf_op jit(solution)/shard_map/psum | solution.py:106
  7.2 4.3 copy-start.5
  27.8 0.8 copy-start.14
  27.8 0.8 copy-start.17
  27.8 0.8 copy-start.18
  27.8 1.3 copy-start.4
  27.8 2.0 copy-start.12
  27.9 239.1 %all-gather.2.cloned.1.call-start = ((), (), s32[]{:S(2)}) async-start(), calls=%async_computation.6 | async-start | bytes 17825792 | tf_op jit(solution)/shard_map/all_gather | solution.py:119
  173.3 5.9 copy-start.6
  179.2 7.5 %copy-start.15 = (bf16[4096,128]{1,0:T(8,128)(2,1)S(1)}, bf16[4096,128]{1,0:T(8,128)(2,1)}, u32[]{:S(2)}) copy-start(bf16[4096,128]{1,0:T(8,128)(2,1)} %param.22) | copy-start | bytes 3145732
  184.6 2.1 copy-start.2
  187.9 93.6 %copy-start.16 = (bf16[4096,128]{1,0:T(8,128)(2,1)S(1)}, bf16[4096,128]{1,0:T(8,128)(2,1)}, u32[]{:S(2)}) copy-start(bf16[4096,128]{1,0:T(8,128)(2,1)} %param.23) | copy-start | bytes 3145732
  276.1 15.8 %all-to-all-start = ((bf16[128,16,128]{2,0,1:T(8,128)(2,1)}), bf16[128,16,128]{2,0,1:T(8,128)(2,1)S(1)}, u32[]{:S(2)}, u32[]{:S(2)}) async-start(bf16[128,16,128]{2,0,1:T(8,128)(2,1)} %bitcast.84), calls=%async_computation | async-start | bytes 1048576 | tf_op jit(solution)/shard_map/all_to_all | solution.py:123
  291.9 14.4 %all-to-all-start.2 = ((bf16[128,16,128]{2,0,1:T(8,128)(2,1)}), bf16[128,16,128]{2,0,1:T(8,128)(2,1)S(1)}, u32[]{:S(2)}, u32[]{:S(2)}) async-start(bf16[128,16,128]{2,0,1:T(8,128)(2,1)} %copy_bitcast_fusion), calls=%async_computation.2 | async-start | bytes 1048576 | tf_op jit(solution)/shard_map/all_to_all | solution.py:124
  295.5 136.9 %reduce-scatter.2.cloned.1.call-start = ((), (), s32[]{:S(2)}) async-start(), calls=%async_computation.7 | async-start | bytes 17825792 | tf_op jit(solution)/shard_map/reduce_scatter | solution.py:137
  295.9 12.7 %copy-start.19 = (bf16[2,256,128]{2,0,1:T(2,128)(2,1)}, bf16[2,256,128]{2,0,1:T(2,128)(2,1)S(1)}, u32[]{:S(2)}) copy-start(bf16[2,256,128]{2,0,1:T(2,128)(2,1)S(1)} %convolution_convert_fusion.9) | copy-start | bytes 393220
  306.3 2.3 copy-start.13
  306.3 2.4 copy-start.8
  327.0 8.3 %copy-start.7 = (bf16[128,16,128]{0,2,1:T(8,128)(2,1)}, bf16[128,16,128]{0,2,1:T(8,128)(2,1)S(1)}, u32[]{:S(2)}) copy-start(bf16[128,16,128]{0,2,1:T(8,128)(2,1)S(1)} %copy.91) | copy-start | bytes 1572868
  335.3 248.7 %all-reduce.6.cloned.1.call-start = ((), (), s32[]{:S(2)}) async-start(), calls=%async_computation.8 | async-start | bytes 6291456 | tf_op jit(solution)/shard_map/psum | solution.py:161
  336.6 3.0 copy-start.3
  344.2 88.2 %copy-start.9 = (f32[2,1024,256]{1,2,0:T(8,128)S(1)}, f32[2,1024,256]{1,2,0:T(8,128)}, u32[]{:S(2)}) copy-start(f32[2,1024,256]{1,2,0:T(8,128)} %get-tuple-element.21) | copy-start | bytes 6291460
  344.2 88.2 %copy-start.20 = (bf16[2,256,128]{2,0,1:T(2,128)(2,1)S(1)}, bf16[2,256,128]{2,0,1:T(2,128)(2,1)}, u32[]{:S(2)}) copy-start(bf16[2,256,128]{2,0,1:T(2,128)(2,1)} %copy-done.19) | copy-start | bytes 393220
  584.0 2.9 copy-start.11
  584.0 4.4 copy-start.10
  586.9 2.9 copy-start.1
Sparse Core Ops, SparseCore 0:
  28.0 145.2 all-reduce.3
  175.0 91.9 all-gather.1
  335.4 96.8 reduce-scatter.1
  435.5 148.4 all-reduce.5
where the time goes:
time: 599 us; the launch traced here: 596 us
  waiting for transfers between devices  445 us (74%)
  matrix products  64.5 us (11%)
  blocking collectives  29.4 us (5%)
  other arithmetic  24.8 us (4%)
  between operations  14.1 us (2%)
  local copies, waits for them, and re-layouts  9.99 us (2%)
  starting transfers between devices  8.88 us (1%)
    psum x1, waiting for transfers between devices, local(): ff_total = lax.psum(term_rows, 'fsdp')  143 us
    psum x1, waiting for transfers between devices, local(): lax.psum(query_grad_rows, 'dp').astype(jnp.float32)  119 us
    reduce_scatter x1, waiting for transfers between devices, local(): lax.psum_scatter(lax.dot_general(normalized_latent_rows, grad_query_tok,...  88.1 us
    all_gather x1, waiting for transfers between devices, local(): query_full = lax.all_gather(w_query, 'fsdp', axis=0, tiled=True)  79 us
    all_to_all x1, blocking collectives, local(): lax.all_to_all(grad_query_heads, 'fsdp', split_axis=0, concat_axis=1, til...  15.1 us
    all_to_all x1, blocking collectives, local(): lax.all_to_all(attn_heads.astype(jnp.bfloat16), 'fsdp', split_axis=0, con...  14.3 us
  transfers between devices with their start and end apart: 6, of which 6 were waited for; matrix products, arithmetic and copies ran while one was open for 8% of the time, Pallas kernels for 0%

commit v1 on v0

v1 whole, which is shorter than its diff:
```python
import functools
import math

import jax
import jax.numpy as jnp
from jax import lax
from jax.experimental import pallas as pl
from jax.experimental.pallas import tpu as pltpu
from jax.sharding import PartitionSpec as P

HD = 128
LCAP = 256
BF = jnp.bfloat16
F32 = jnp.float32
MESH = pl.DeviceIdType.MESH


def coords():
    d, f = lax.axis_index("dp"), lax.axis_index("fsdp")
    return d // 2, d % 2, f // 8, (f // 2) % 4, f % 2


def device(y, zh, zl, x, c):
    return (y * 2 + zh, zl * 8 + x * 2 + c)


def x_peers(y, zh, zl, x, c):
    return [(device(y, zh, zl, (x + k) % 4, c), (x + k) % 4) for k in (1, 2, 3)]


def y_peers(y, zh, zl, x, c):
    return [(device((y + k) % 4, zh, zl, x, c), (y + k) % 4) for k in (1, 2, 3)]


def z_peers(y, zh, zl, x, c):
    z = zh * 2 + zl
    there = [(z + k) % 4 for k in (1, 2, 3)]
    return [(device(y, t // 2, t % 2, x, c), t) for t in there]


def dp_peers(y, zh, zl, x, c):
    there = [((y + k) % 4, (zh + a) % 2) for a in (0, 1) for k in range(4) if a or k]
    return [(device(v, w, zl, x, c), v * 2 + w) for v, w in there]


def chip_peers(y, zh, zl, x, c):
    there = [((zl + a) % 2, (x + k) % 4) for a in (0, 1) for k in range(4) if a or k]
    return [(device(y, zh, w, v, c), w * 4 + v) for w, v in there]


def quad_peers(y, zh, zl, x, c):
    there = [((zl + a) % 2, (c + b) % 2) for a in (0, 1) for b in (0, 1) if a or b]
    return [(device(y, zh, w, x, b), w * 2 + b) for w, b in there]


def core_peer(y, zh, zl, x, c):
    return [(device(y, zh, zl, x, 1 - c), 1 - c)]


def span(index, size):
    return pl.ds(pl.multiple_of(index * size, size), size)


class Sender:
    def __init__(self, send_sem, recv_sem):
        self.sems, self.count, self.open = (send_sem, recv_sem), 0, []

    def send(self, src, dst, to):
        t = self.count
        self.count += 1
        if to is None:
            copy = pltpu.make_async_copy(src, dst, self.sems[0].at[t])
        else:
            copy = pltpu.make_async_remote_copy(
                src_ref=src,
                dst_ref=dst,
                send_sem=self.sems[0].at[t],
                recv_sem=self.sems[1].at[t],
                device_id=to,
                device_id_type=MESH,
            )
        copy.start()
        self.open.append((copy, to is None))
        return copy

    def finish(self, landed=()):
        for copy, own in self.open:
            if own:
                copy.wait()
            elif any(copy is other for other in landed):
                copy.wait_send()
            else:
                copy.wait()


def exchange(name, cid, copies, body, groups, outs, *ins):
    def kernel(*refs):
        in_refs, out_refs = refs[: len(ins)], refs[len(ins) : len(ins) + len(outs)]
        place = coords()
        barrier = pltpu.get_barrier_semaphore()
        peers = [to for group in groups for to, _ in group(*place)]
        for to in peers:
            pl.semaphore_signal(barrier, inc=1, device_id=to, device_id_type=MESH)
        pl.semaphore_wait(barrier, len(peers))
        sender = Sender(refs[-2], refs[-1])
        landed = body(sender, place, in_refs, out_refs)
        assert sender.count == copies, sender.count
        sender.finish(landed or ())

    return pl.pallas_call(
        kernel,
        out_shape=[jax.ShapeDtypeStruct(shape, BF) for shape in outs],
        in_specs=[pl.BlockSpec(memory_space=pl.ANY)] * len(ins),
        out_specs=[pl.BlockSpec(memory_space=pl.ANY)] * len(outs),
        scratch_shapes=[
            pltpu.SemaphoreType.DMA((copies,)),
            pltpu.SemaphoreType.DMA((copies,)),
        ],
        compiler_params=pltpu.CompilerParams(collective_id=cid, has_side_effects=True),
        name=name,
    )(*ins)


def first_body(s, place, ins, outs):
    xn, go, w = ins
    xs, gs, wx = outs
    y, zh, zl, x, c = place
    mine = zl * 2 + c
    pair = core_peer(*place)[0][0]
    across = device(y, zh, 1 - zl, x, c)
    over = s.send(w, wx.at[span(mine, 256)], across)
    for to, v in x_peers(*place) + [(None, x)]:
        for half in (0, 1):
            s.send(
                xn.at[:, span(half * 4 + v, 512)],
                xs.at[span(x, 128), pl.ds(half * 512, 512)],
                to,
            )
            s.send(
                go.at[:, span(half * 4 + v, 256)],
                gs.at[span(x, 128), pl.ds(half * 256, 256)],
                to,
            )
    s.send(w, wx.at[span(mine, 256)], pair)
    s.send(w, wx.at[span(mine, 256)], None)
    over.wait_recv()
    theirs = (1 - zl) * 2 + c
    s.send(wx.at[span(theirs, 256)], wx.at[span(theirs, 256)], pair)
    return (over,)


def core_body(s, place, ins, outs):
    c = place[4]
    s.send(ins[0].at[1 - c], outs[0], core_peer(*place)[0][0])


def scatter_body(s, place, ins, outs):
    ff, qp = ins
    fr, qr = outs
    y, zh, zl, x, c = place
    here = zl * 4 + x
    for to, j in chip_peers(*place) + [(None, here)]:
        s.send(ff.at[j], fr.at[here], to)
    for to, v in x_peers(*place) + [(None, x)]:
        s.send(qp.at[:, span(v, 512)], qr.at[x], to)


def caption_body(s, place, ins, outs):
    (rows,) = ins
    (full,) = outs
    y, zh, zl, x, c = place
    here = zl * 4 + x
    pair = core_peer(*place)[0][0]
    coming = []
    for a in (0, 1):
        for k in (1, 3, 2, 0):
            if a or k:
                to = device(y, zh, (zl + a) % 2, (x + k) % 4, c)
                coming.append(
                    (s.send(rows, full.at[c, here], to), ((zl + a) % 2) * 4 + (x + 4 - k) % 4)
                )
    s.send(rows, full.at[c, here], pair)
    s.send(rows, full.at[c, here], None)
    for copy, j in coming:
        copy.wait_recv()
        s.send(full.at[c, j], full.at[c, j], pair)
    return tuple(copy for copy, _ in coming)


def quad_body(s, place, ins, outs):
    (sel,) = ins
    (kv,) = outs
    y, zh, zl, x, c = place
    here = zl * 2 + c
    for to, q in quad_peers(*place) + [(None, here)]:
        s.send(sel.at[q // 2], kv.at[here], to)


def attn_back_body(s, place, ins, outs):
    attn, gkv = ins
    tok, parts = outs
    y, zh, zl, x, c = place
    here = zl * 2 + c
    for to, q in quad_peers(*place) + [(None, here)]:
        s.send(gkv.at[q], parts.at[here], to)
    for to, v in x_peers(*place) + [(None, x)]:
        for half in (0, 1):
            s.send(
                attn.at[span(v, 128), pl.ds(half * 256, 256)],
                tok.at[:, span(half * 4 + x, 256)],
                to,
            )


def gather_body(s, place, ins, outs):
    gq, kvp = ins
    gqa, kvr = outs
    y, zh, zl, x, c = place
    here = y * 2 + zh
    for to, v in x_peers(*place) + [(None, x)]:
        s.send(gq, gqa.at[:, span(x, 512)], to)
    for to, j in dp_peers(*place) + [(None, here)]:
        s.send(kvp.at[j], kvr.at[here], to)


def grads_body(s, place, ins, outs):
    dxn, part, kvs = ins
    dtok, r1, r2, kva = outs
    y, zh, zl, x, c = place
    z = zh * 2 + zl
    here = y * 2 + zh
    for to, v in y_peers(*place) + [(None, y)]:
        s.send(part.at[:, v, :, :, pl.ds(0, 1024)], r1.at[y], to)
    for to, t in z_peers(*place) + [(None, z)]:
        s.send(part.at[t % 2, :, t // 2, :, pl.ds(1024, 1024)], r2.at[z], to)
    for to, v in x_peers(*place) + [(None, x)]:
        for half in (0, 1):
            s.send(
                dxn.at[span(v, 128), pl.ds(half * 512, 512)],
                dtok.at[:, span(half * 4 + x, 512)],
                to,
            )
    for to, j in dp_peers(*place) + [(None, here)]:
        s.send(kvs, kva.at[here], to)


def second_body(s, place, ins, outs):
    s1, s2 = ins
    r1, r2 = outs
    y, zh, zl, x, c = place
    z = zh * 2 + zl
    for to, t in z_peers(*place) + [(None, z)]:
        s.send(s1.at[t % 2, t // 2], r1.at[z], to)
    for to, v in y_peers(*place) + [(None, y)]:
        s.send(s2.at[v], r2.at[y], to)


def last_body(s, place, ins, outs):
    y, zh, zl, x, c = place
    here = y * 2 + zh
    for to, j in dp_peers(*place) + [(None, here)]:
        s.send(ins[0], outs[0].at[here], to)


def attend_kernel(live_ref, q_ref, g_ref, kv_ref, attn_ref, gq_ref, gkv_ref):
    inv_root = 1.0 / math.sqrt(HD)
    q, g = q_ref[...], g_ref[...]
    k, v = kv_ref[0, :, :HD], kv_ref[0, :, HD:]
    nt = (((1,), (1,)), ((), ()))
    tn = (((0,), (0,)), ((), ()))
    scores = lax.dot_general(q, k, nt, preferred_element_type=F32) * inv_root
    live = lax.broadcasted_iota(jnp.int32, scores.shape, 1) < live_ref[0]
    scores = jnp.where(live, scores, -1e30)
    e = jnp.exp(scores - jnp.max(scores, axis=-1, keepdims=True))
    probs = e / jnp.sum(e, axis=-1, keepdims=True)
    probs_b = probs.astype(BF)
    attn_ref[...] = jnp.dot(probs_b, v, preferred_element_type=F32).astype(BF)
    gp = lax.dot_general(g, v, nt, preferred_element_type=F32)
    gs = (probs * (gp - jnp.sum(probs * gp, axis=-1, keepdims=True))).astype(BF)
    gq_ref[...] = (jnp.dot(gs, k, preferred_element_type=F32) * inv_root).astype(BF)
    gk = lax.dot_general(gs, q, tn, preferred_element_type=F32) * inv_root
    gv = lax.dot_general(probs_b, g, tn, preferred_element_type=F32)
    gkv_ref[0, :, :HD] = gk.astype(BF)
    gkv_ref[0, :, HD:] = gv.astype(BF)


def attend(live, q, g, kv):
    rows = q.shape[0]
    col = pl.BlockSpec((rows, HD), lambda h: (0, h))
    per = pl.BlockSpec((1, LCAP, 2 * HD), lambda h: (h, 0, 0))
    return pl.pallas_call(
        attend_kernel,
        grid=(4,),
        out_shape=[
            jax.ShapeDtypeStruct(q.shape, BF),
            jax.ShapeDtypeStruct(q.shape, BF),
            jax.ShapeDtypeStruct(kv.shape, BF),
        ],
        in_specs=[pl.BlockSpec(memory_space=pltpu.SMEM), col, col, per],
        out_specs=[col, col, per],
        compiler_params=pltpu.CompilerParams(vmem_limit_bytes=32 * 2**20),
        name="attend",
    )(live, q, g, kv)


def rms_scale(values, gain):
    work = values.astype(F32)
    return (
        work
        * lax.rsqrt(jnp.mean(work * work, axis=-1, keepdims=True) + 1e-06)
        * gain.astype(F32)
    )


def local(
    cap_hidden,
    t5_norm_gain,
    t5_wi0,
    t5_wi1,
    t5_wo,
    t5_final_gain,
    cap_lengths,
    latents,
    w_query,
    w_key,
    w_value,
    caption_of_image,
    grad_out,
):
    y, zh, zl, x, c = coords()

    lat = latents.astype(F32)
    removed = lat - jnp.mean(lat, axis=-1, keepdims=True)
    rstd = lax.rsqrt(jnp.mean(removed * removed, axis=-1, keepdims=True) + 1e-06)
    xhat = removed * rstd
    xn = xhat.astype(BF)
    wq = w_query.reshape(256, 2, 4, 256).transpose(0, 2, 1, 3).reshape(256, 2048)
    xs, gs, wx = exchange(
        "tokens_to_features",
        0,
        20,
        first_body,
        (x_peers, quad_peers),
        [(512, 1024), (512, 512), (1024, 2048)],
        xn,
        grad_out,
        wq,
    )

    normed = rms_scale(cap_hidden, t5_norm_gain).astype(BF)
    gate = jnp.dot(normed, t5_wi0, preferred_element_type=F32)
    lift = jnp.dot(normed, t5_wi1, preferred_element_type=F32)
    hidden = (jax.nn.gelu(gate, approximate=True) * lift).astype(BF)
    term = jnp.dot(hidden, t5_wo, preferred_element_type=F32).astype(BF)
    term = term.reshape(2, 256, 4096)
    (other,) = exchange(
        "ff_core_pair", 1, 1, core_body, (core_peer,), [(256, 4096)], term
    )
    own = lax.dynamic_index_in_dim(term, c, 0, keepdims=False)
    ff_pair = (own.astype(F32) + other.astype(F32)).astype(BF)
    q_part = jnp.dot(xs, wx, preferred_element_type=F32).astype(BF)

    ff_blocks, q_blocks = exchange(
        "ff_and_query_scatter",
        2,
        12,
        scatter_body,
        (chip_peers,),
        [(8, 32, 4096), (4, 512, 512)],
        ff_pair.reshape(8, 32, 4096),
        q_part,
    )
    ff_rows = jnp.sum(ff_blocks.astype(F32), axis=0)
    row = c * 256 + (zl * 4 + x) * 32
    cap_rows = lax.dynamic_slice_in_dim(cap_hidden, row, 32, 0)
    caption_rows = rms_scale(cap_rows.astype(F32) + ff_rows, t5_final_gain).astype(BF)
    queries = jnp.sum(q_blocks.astype(F32), axis=0).astype(BF)

    (caption,) = exchange(
        "caption_gather",
        3,
        16,
        caption_body,
        (chip_peers, core_peer),
        [(2, 8, 32, 4096)],
        caption_rows,
    )
    caption = caption.reshape(512, 4096)
    keys = jnp.dot(caption, w_key, preferred_element_type=F32).astype(BF)
    values = jnp.dot(caption, w_value, preferred_element_type=F32).astype(BF)
    key_value = jnp.concatenate([keys, values], axis=1).reshape(2, LCAP, 256)
    chosen = caption_of_image[:, None, None] == 0
    selected = jnp.where(chosen, key_value[:1], key_value[1:])
    (kv,) = exchange(
        "keys_to_heads", 4, 4, quad_body, (quad_peers,), [(4, LCAP, 256)], selected
    )

    mine = lax.dynamic_index_in_dim(caption_of_image, zl, 0)
    live = jnp.where(mine == 0, cap_lengths[:1], cap_lengths[1:])
    attn, gq, gkv = attend(live, queries, gs, kv)

    attn_tok, gkv_parts = exchange(
        "attn_to_tokens",
        5,
        12,
        attn_back_body,
        (x_peers, quad_peers),
        [(128, 2048), (4, LCAP, 256)],
        attn,
        gkv,
    )
    attn_out = attn_tok.astype(F32)
    per_image = jnp.sum(gkv_parts.reshape(2, 2, LCAP, 256).astype(F32), axis=1)
    grad_kv = jnp.stack(
        [
            jnp.sum(jnp.where(caption_of_image[:, None, None] == i, per_image, 0.0), axis=0)
            for i in (0, 1)
        ]
    )
    grad_kv = grad_kv.astype(BF).reshape(512, 256)
    kv_part = lax.dot_general(
        caption, grad_kv, (((0,), (0,)), ((), ())), preferred_element_type=F32
    ).astype(BF)

    gq_all, kv_blocks = exchange(
        "grad_query_gather",
        6,
        12,
        gather_body,
        (x_peers, dp_peers),
        [(512, 2048), (8, 512, 256)],
        gq,
        kv_part.reshape(8, 512, 256),
    )
    kv_sum = jnp.sum(kv_blocks.astype(F32), axis=0).astype(BF)
    dxn = lax.dot_general(
        gq_all, wx, (((1,), (1,)), ((), ())), preferred_element_type=F32
    ).astype(BF)
    q_grad = lax.dot_general(
        xs, gq_all, (((0,), (0,)), ((), ())), preferred_element_type=F32
    ).astype(BF)
    q_grad = q_grad.reshape(2, 2, 256, 2048).transpose(1, 0, 2, 3)
    (other,) = exchange(
        "grad_query_core_pair", 7, 1, core_body, (core_peer,), [(2, 256, 2048)], q_grad
    )
    own = lax.dynamic_index_in_dim(q_grad, c, 0, keepdims=False)
    pair = (own.astype(F32) + other.astype(F32)).astype(BF).reshape(2, 4, 2, 32, 2048)

    dtok, r1, r2, kv_all = exchange(
        "grads_scatter",
        8,
        24,
        grads_body,
        (x_peers, y_peers, z_peers, dp_peers),
        [(128, 4096), (4, 2, 2, 32, 1024), (4, 4, 32, 1024), (8, 512, 256)],
        dxn,
        pair,
        kv_sum,
    )
    s1 = jnp.sum(r1.astype(F32), axis=0).astype(BF)
    s2 = jnp.sum(r2.astype(F32), axis=0).astype(BF)
    t1, t2 = exchange(
        "grad_query_scatter",
        9,
        8,
        second_body,
        (y_peers, z_peers),
        [(4, 32, 1024), (4, 32, 1024)],
        s1,
        s2,
    )
    block = jnp.concatenate(
        [jnp.sum(t1.astype(F32), axis=0), jnp.sum(t2.astype(F32), axis=0)], axis=1
    ).astype(BF)
    (q_full,) = exchange(
        "grad_query_spread", 10, 8, last_body, (dp_peers,), [(8, 32, 2048)], block
    )

    grad_xn = dtok.astype(F32)
    latent_token_gradient = rstd * (
        grad_xn
        - jnp.mean(grad_xn, axis=-1, keepdims=True)
        - xhat * jnp.mean(grad_xn * xhat, axis=-1, keepdims=True)
    )
    grad_query = (
        q_full.reshape(256, 4, 2, 256).transpose(0, 2, 1, 3).reshape(256, 2048).astype(F32)
    )
    kv_all = kv_all.reshape(4096, 256).astype(F32)
    return (attn_out, latent_token_gradient, grad_query, kv_all[:, :128], kv_all[:, 128:])


def solution(mesh):
    placed = (
        P("dp", None),
        P(),
        P(None, "fsdp"),
        P(None, "fsdp"),
        P("fsdp", None),
        P(),
        P("dp"),
        P(("dp", "fsdp"), None),
        P("fsdp", None),
        P(None, "fsdp"),
        P(None, "fsdp"),
        P("dp"),
        P(("dp", "fsdp"), None),
    )
    return jax.shard_map(
        local,
        mesh=mesh,
        in_specs=placed,
        out_specs=(
            P(("dp", "fsdp"), None),
            P(("dp", "fsdp"), None),
            P("fsdp", None),
            P(None, "fsdp"),
            P(None, "fsdp"),
        ),
        check_vma=False,
    )
```

time: 599 us -> 391 us (0.65)
  waiting for transfers between devices: 445 us -> 0 us
  Pallas kernels: 0 us -> 286 us
  blocking collectives: 29.4 us -> 0 us
  matrix products: 64.5 us -> 40 us
  local copies, waits for them, and re-layouts: 9.99 us -> 23 us
  other arithmetic: 24.8 us -> 37.8 us
  between operations: 14.1 us -> 3.12 us
  starting transfers between devices: 8.88 us -> 0 us
    pallas_call x0 -> x12, Pallas kernels: none -> 286 us  [the longest x11 282 us: exchange(): pl.pallas_call(kernel, out_shape=[jax.ShapeDtypeStruct(shape, BF) for sha...]
    psum x2 -> x0, waiting for transfers between devices: 262 us -> none  [the longest x1 143 us: local(): ff_total = lax.psum(term_rows, 'fsdp')]
    reduce_scatter x1 -> x0, waiting for transfers between devices: 88.1 us -> none  [local(): lax.psum_scatter(lax.dot_general(normalized_latent_rows, grad_query_tok,...]
    all_gather x1 -> x0, waiting for transfers between devices: 79 us -> none  [local(): query_full = lax.all_gather(w_query, 'fsdp', axis=0, tiled=True)]
    all_to_all x2 -> x0, blocking collectives: 29.4 us -> none  [the longest x1 15.1 us: local(): lax.all_to_all(grad_query_heads, 'fsdp', split_axis=0, concat_axis=1, til...]
    dot_general x18 -> x8, matrix products: 62.3 us -> 40 us  [the longest x1 9.75 us: local(): term = jnp.dot(hidden, t5_wo, preferred_element_type=F32).astype(BF)]
    all_to_all x2 -> x0, waiting for transfers between devices: 15.2 us -> none  [the longest x1 8.22 us: local(): lax.all_to_all(grad_out, 'fsdp', split_axis=1, concat_axis=0, tiled=True)]
    reduce_sum x3 -> x12, other arithmetic: 0.74 us -> 11.6 us  [the longest x1 2.33 us: local(): queries = jnp.sum(q_blocks.astype(F32), axis=0).astype(BF)]
  transfers between devices with their start and end apart: 6 -> 0, of which waited for: 6 -> 0; matrix products, arithmetic and copies ran while one was open for 8% -> 0% of each run, Pallas kernels for 0% -> 0%
where the time goes in v1:
time: 391 us; the launch traced here: 390 us
  Pallas kernels  286 us (73%)
  matrix products  40 us (10%)
  other arithmetic  37.8 us (10%)
  local copies, waits for them, and re-layouts  23 us (6%)
    pallas_call x11, Pallas kernels, exchange(): pl.pallas_call(kernel, out_shape=[jax.ShapeDtypeStruct(shape, BF) for sha...  282 us
    dot_general x1, matrix products, local(): term = jnp.dot(hidden, t5_wo, preferred_element_type=F32).astype(BF)  9.75 us
    convert_element_type x3, local copies, waits for them, and re-layouts, local(): q_full.reshape(256, 4, 2, 256).transpose(0, 2, 1, 3).reshape(256, 2048)  8.55 us

profile of v1, /device:TPU:0, one launch (start us, length us, event | category | flops | bytes accessed | tf_op | source)
XLA Modules:
  0.0 390.3 jit_solution(17693147047451345863)
XLA Ops:
  0.7 1.4 dynamic_slice.13
  2.8 1.4 fusion.31
  6.1 3.1 fusion
  9.2 5.2 %fusion.23 = f32[512,384]{1,0:T(8,128)} fusion(bf16[4096,384]{1,0:T(8,128)(2,1)} %param.15, bf16[512,4096]{1,0:T(8,128)(2,1)S(1)} %copy-done.10, f32[4096]{0:T(1024)S(1)} %convert_element_type.132, f32[512]{0:T(512)S(1)} %add_rsqrt_fusion), kind=kOutput, calls=%fused_computation.43 | convolution fusion | flops 1620574208 | bytes 8144896 | tf_op jit(solution)/shard_map/dot_general | solution.py:351
  14.5 9.8 %convolution_convert_fusion = bf16[512,4096]{1,0:T(8,128)(2,1)} fusion(bf16[384,4096]{1,0:T(8,128)(2,1)S(1)} %copy-done, f32[512,384]{1,0:T(8,128)} %fusion.23, bf16[4096,384]{1,0:T(8,128)(2,1)} %param.16, bf16[512,4096]{1,0:T(8,128)(2,1)} %param.13, f32[4096]{0:T(1024)S(1)} %convert_element_type.132, f32[512]{0:T(512)S(1)} %add_rsqrt_fusion), kind=kOutput, calls=%fused_computation.5 | convolution fusion | flops 3232104448 | bytes 15484928 | tf_op jit(solution)/shard_map/dot_general | solution.py:354
  24.2 4.5 %ff_core_pair.1 = bf16[256,4096]{1,0:T(8,128)(2,1)} custom-call(bf16[2,256,4096]{2,1,0:T(8,128)(2,1)} %bitcast.50), custom_call_target="tpu_custom_call" | custom-call | tf_op jit(solution)/shard_map/ff_core_pair/pallas_call | solution.py:110
  28.8 4.4 %fusion.4 = bf16[256,4096]{1,0:T(8,128)(2,1)} fusion(bf16[256,4096]{1,0:T(8,128)(2,1)} %ff_core_pair.1, bf16[2,256,4096]{2,1,0:T(8,128)(2,1)} %bitcast.51, s32[]{:T(128)S(6)} %select_n.50), kind=kLoop, calls=%fused_computation.10 | loop fusion | flops 4194304 | bytes 6291460 | tf_op jit(solution)/shard_map/convert_element_type | solution.py:360
  33.9 1.3 fusion.8.refs_0_
  36.0 1.1 copy.31
  37.1 1.6 reshape.111.refs_2_
  38.7 48.2 %tokens_to_features.1 = (bf16[512,1024]{1,0:T(8,128)(2,1)}, bf16[512,512]{1,0:T(8,128)(2,1)}, bf16[1024,2048]{1,0:T(8,128)(2,1)}) custom-call(bf16[128,4096]{1,0:T(8,128)(2,1)} %fusion.8.refs_0_, bf16[128,2048]{1,0:T(8,128)(2,1)} %refs_1_.1, bf16[256,2048]{1,0:T(8,128)(2,1)} %reshape.111.refs_2_), custom_call_target="tpu_custom_call" | custom-call | tf_op jit(solution)/shard_map/tokens_to_features/pallas_call | solution.py:110
  87.0 6.2 %convolution_convert_fusion.3.refs_1_ = bf16[512,2048]{1,0:T(8,128)(2,1)} fusion(bf16[512,1024]{1,0:T(8,128)(2,1)} %get-tuple-element.23, bf16[1024,2048]{1,0:T(8,128)(2,1)} %get-tuple-element.24), kind=kOutput, calls=%fused_computation.16 | convolution fusion | flops 2148532224 | bytes 7340032 | tf_op jit(solution)/shard_map/dot_general | solution.py:361
  93.1 55.6 %ff_and_query_scatter.1 = (bf16[8,32,4096]{2,1,0:T(8,128)(2,1)}, bf16[4,512,512]{2,1,0:T(8,128)(2,1)}) custom-call(bf16[8,32,4096]{2,1,0:T(8,128)(2,1)} %bitcast.52, bf16[512,2048]{1,0:T(8,128)(2,1)} %convolution_convert_fusion.3.refs_1_), custom_call_target="tpu_custom_call" | custom-call | tf_op jit(solution)/shard_map/ff_and_query_scatter/pallas_call | solution.py:110
  148.7 2.3 reduce_sum.159.q_ref
  151.5 1.2 multiply_reduce_fusion
  152.7 1.8 multiply_convert_fusion.refs_0_
  154.5 35.2 %caption_gather.1 = bf16[2,8,32,4096]{3,2,1,0:T(8,128)(2,1)} custom-call(bf16[32,4096]{1,0:T(8,128)(2,1)} %multiply_convert_fusion.refs_0_), custom_call_target="tpu_custom_call" | custom-call | tf_op jit(solution)/shard_map/caption_gather/pallas_call | solution.py:110
  189.7 3.8 convolution_convert_fusion.6
  193.6 1.5 convolution_convert_fusion.5
  195.3 0.8 broadcast_select_fusion.refs_0_
  196.1 8.5 %keys_to_heads.1.kv_ref = bf16[4,256,256]{2,1,0:T(8,128)(2,1)} custom-call(bf16[2,256,256]{2,1,0:T(8,128)(2,1)} %broadcast_select_fusion.refs_0_), custom_call_target="tpu_custom_call" | custom-call | tf_op jit(solution)/shard_map/keys_to_heads/pallas_call | solution.py:110
  204.7 1.0 copy-done.2
  205.7 4.3 %attend.1 = (bf16[512,512]{1,0:T(8,128)(2,1)S(1)}, bf16[512,512]{1,0:T(8,128)(2,1)S(1)}, bf16[4,256,256]{2,1,0:T(8,128)(2,1)S(1)}) custom-call(s32[1]{0:T(128)S(6)} %select_n.48.live_ref, bf16[512,512]{1,0:T(8,128)(2,1)S(1)} %reduce_sum.159.q_ref, bf16[512,512]{1,0:T(8,128)(2,1)S(1)} %copy-done.4, bf16[4,256,256]{2,1,0:T(8,128)(2,1)S(1)} %copy-done.2), custom_call_target="tpu_custom_call" | custom-call | tf_op jit(solution)/shard_map/attend/pallas_call | solution.py:291
  212.5 11.4 %attn_to_tokens.1 = (bf16[128,2048]{1,0:T(8,128)(2,1)}, bf16[4,256,256]{2,1,0:T(8,128)(2,1)}) custom-call(bf16[512,512]{1,0:T(8,128)(2,1)} %copy-done.5, bf16[4,256,256]{2,1,0:T(8,128)(2,1)} %copy-done.6), custom_call_target="tpu_custom_call" | custom-call | tf_op jit(solution)/shard_map/attn_to_tokens/pallas_call | solution.py:110
  223.9 2.1 convert_element_type.149
  226.0 1.2 convert_reduce_fusion.3
  227.3 4.8 %convolution_convert_fusion.1 = bf16[4096,256]{1,0:T(8,128)(2,1)} fusion(bf16[512,4096]{1,0:T(8,128)(2,1)} %bitcast.47, bf16[512,256]{1,0:T(8,128)(2,1)S(1)} %bitcast.60), kind=kOutput, calls=%fused_computation.6 | convolution fusion | flops 1074790400 | bytes 6553600 | tf_op jit(solution)/shard_map/dot_general | solution.py:421
  232.1 37.4 %grad_query_gather.1 = (bf16[512,2048]{1,0:T(8,128)(2,1)}, bf16[8,512,256]{2,1,0:T(8,128)(2,1)}) custom-call(bf16[512,512]{1,0:T(8,128)(2,1)} %copy-done.3, bf16[8,512,256]{2,1,0:T(8,128)(2,1)} %bitcast.57), custom_call_target="tpu_custom_call" | custom-call | tf_op jit(solution)/shard_map/grad_query_gather/pallas_call | solution.py:110
  269.5 6.3 %convolution_convert_fusion.4.refs_0_ = bf16[512,1024]{1,0:T(8,128)(2,1)} fusion(bf16[512,2048]{1,0:T(8,128)(2,1)} %get-tuple-element.33, bf16[1024,2048]{1,0:T(8,128)(2,1)} %get-tuple-element.24), kind=kOutput, calls=%fused_computation.28 | convolution fusion | flops 2148007936 | bytes 7340032 | tf_op jit(solution)/shard_map/dot_general | solution.py:436
  275.9 2.4 convolution_convert_fusion.2
  278.2 2.2 copy.32
  280.5 4.5 %grad_query_core_pair.1 = bf16[2,256,2048]{2,1,0:T(8,128)(2,1)} custom-call(bf16[2,2,256,2048]{3,2,1,0:T(8,128)(2,1)} %bitcast.49), custom_call_target="tpu_custom_call" | custom-call | tf_op jit(solution)/shard_map/grad_query_core_pair/pallas_call | solution.py:110
  285.0 4.6 %fusion.3 = bf16[2,256,2048]{2,1,0:T(8,128)(2,1)} fusion(bf16[2,256,2048]{2,1,0:T(8,128)(2,1)} %grad_query_core_pair.1, bf16[2,2,256,2048]{3,2,0,1:T(8,128)(2,1)} %copy.32, s32[]{:T(128)S(6)} %select_n.50), kind=kLoop, calls=%fused_computation.8 | loop fusion | flops 4194304 | bytes 6291460 | tf_op jit(solution)/shard_map/convert_element_type | solution.py:447
  289.6 1.0 reduce_sum.165.refs_2_
  290.7 48.8 %grads_scatter.1 = (bf16[128,4096]{1,0:T(8,128)(2,1)}, bf16[4,2,2,32,1024]{4,3,2,1,0:T(8,128)(2,1)}, bf16[4,4,32,1024]{3,2,1,0:T(8,128)(2,1)}, bf16[8,512,256]{2,1,0:T(8,128)(2,1)}) custom-call(bf16[512,1024]{1,0:T(8,128)(2,1)} %convolution_convert_fusion.4.refs_0_, bf16[2,4,2,32,2048]{4,3,2,1,0:T(8,128)(2,1)} %bitcast.53, bf16[512,256]{1,0:T(8,128)(2,1)} %reduce_sum.165.refs_2_), custom_call_target="tpu_custom_call" | custom-call | tf_op jit(solution)/shard_map/grads_scatter/pallas_call | solution.py:110
  339.5 2.1 convert_reduce_fusion.1
  341.6 3.3 fusion.10
  345.0 0.9 reduce_sum.168.refs_0_
  345.9 0.9 reduce_sum.169.refs_1_
  346.8 10.3 %grad_query_scatter.1 = (bf16[4,32,1024]{2,1,0:T(8,128)(2,1)}, bf16[4,32,1024]{2,1,0:T(8,128)(2,1)}) custom-call(bf16[2,2,32,1024]{3,2,1,0:T(8,128)(2,1)} %reduce_sum.168.refs_0_, bf16[4,32,1024]{2,1,0:T(8,128)(2,1)} %reduce_sum.169.refs_1_), custom_call_target="tpu_custom_call" | custom-call | tf_op jit(solution)/shard_map/grad_query_scatter/pallas_call | solution.py:110
  357.1 1.0 reduce.5
  358.1 1.0 reduce.4
  359.8 17.6 %grad_query_spread.1 = bf16[8,32,2048]{2,1,0:T(8,128)(2,1)} custom-call(bf16[32,2048]{1,0:T(8,128)(2,1)} %pad_maximum_fusion.2.refs_0_), custom_call_target="tpu_custom_call" | custom-call | tf_op jit(solution)/shard_map/grad_query_spread/pallas_call | solution.py:110
  377.4 3.4 reshape.121
  380.8 1.9 copy.27
  382.7 3.3 reshape.119
  386.0 2.1 bitcast_convert_fusion
  388.0 2.3 fusion.29
  (61 shorter events, 6.0 us)
Async XLA Ops:
  0.6 13.9 %copy-start = (bf16[384,4096]{1,0:T(8,128)(2,1)S(1)}, bf16[384,4096]{1,0:T(8,128)(2,1)}, u32[]{:S(2)}) copy-start(bf16[384,4096]{1,0:T(8,128)(2,1)} %param.17) | copy-start | bytes 9437188
  0.7 8.6 %copy-start.10 = (bf16[512,4096]{1,0:T(8,128)(2,1)S(1)}, bf16[512,4096]{1,0:T(8,128)(2,1)}, u32[]{:S(2)}) copy-start(bf16[512,4096]{1,0:T(8,128)(2,1)} %param.13) | copy-start | bytes 12582916
  28.8 4.4 %copy-start.8 = (bf16[128,4096]{1,0:T(8,128)(2,1)S(1)}, bf16[128,4096]{1,0:T(8,128)(2,1)}, u32[]{:S(2)}) copy-start(bf16[128,4096]{1,0:T(8,128)(2,1)} %param.20) | copy-start | bytes 3145732
  33.2 2.0 copy-start.17
  93.1 57.9 %copy-start.21 = (s32[2]{0:T(128)S(1)}, s32[2]{0:T(128)}, u32[]{:S(2)}) copy-start(s32[2]{0:T(128)} %param.24) | copy-start | bytes 28
  148.7 2.4 copy-start.12
  148.7 2.7 copy-start.18
  151.5 38.2 %copy-start.13 = (bf16[4096,128]{1,0:T(8,128)(2,1)S(1)}, bf16[4096,128]{1,0:T(8,128)(2,1)}, u32[]{:S(2)}) copy-start(bf16[4096,128]{1,0:T(8,128)(2,1)} %param.22) | copy-start | bytes 3145732
  189.7 3.9 copy-start.7
  189.7 3.9 copy-start.14
  193.6 11.1 %copy-start.4 = (bf16[512,512]{1,0:T(8,128)(2,1)S(1)}, bf16[512,512]{1,0:T(8,128)(2,1)}, u32[]{:S(2)}) copy-start(bf16[512,512]{1,0:T(8,128)(2,1)} %get-tuple-element.26.g_ref) | copy-start | bytes 1572868
  204.7 1.0 copy-start.2
  210.1 0.8 copy-start.3
  210.9 0.8 copy-start.5
  211.7 0.8 copy-start.6
  269.5 6.3 %copy-start.19 = (bf16[512,2048]{1,0:T(8,128)(2,1)S(1)}, bf16[512,2048]{1,0:T(8,128)(2,1)}, u32[]{:S(2)}) copy-start(bf16[512,2048]{1,0:T(8,128)(2,1)} %get-tuple-element.33) | copy-start | bytes 6291460
  269.5 6.3 %copy-start.20 = (bf16[512,1024]{1,0:T(8,128)(2,1)S(1)}, bf16[512,1024]{1,0:T(8,128)(2,1)}, u32[]{:S(2)}) copy-start(bf16[512,1024]{1,0:T(8,128)(2,1)} %get-tuple-element.23) | copy-start | bytes 3145732
  285.0 4.6 %copy-start.11 = (bf16[8,512,256]{2,1,0:T(8,128)(2,1)S(1)}, bf16[8,512,256]{2,1,0:T(8,128)(2,1)}, u32[]{:S(2)}) copy-start(bf16[8,512,256]{2,1,0:T(8,128)(2,1)} %get-tuple-element.34) | copy-start | bytes 6291460
  289.6 49.9 %copy-start.9 = (bf16[128,4096]{1,0:T(8,128)(2,1)S(1)}, bf16[128,4096]{1,0:T(8,128)(2,1)}, u32[]{:S(2)}) copy-start(bf16[128,4096]{1,0:T(8,128)(2,1)} %param.20) | copy-start | bytes 3145732
  339.5 5.5 %copy-start.16 = (bf16[4,2,2,32,1024]{4,3,2,1,0:T(8,128)(2,1)S(1)}, bf16[4,2,2,32,1024]{4,3,2,1,0:T(8,128)(2,1)}, u32[]{:S(2)}) copy-start(bf16[4,2,2,32,1024]{4,3,2,1,0:T(8,128)(2,1)} %get-tuple-element.36) | copy-start | bytes 3145732
  341.6 4.3 %copy-start.15 = (bf16[4,4,32,1024]{3,2,1,0:T(8,128)(2,1)S(1)}, bf16[4,4,32,1024]{3,2,1,0:T(8,128)(2,1)}, u32[]{:S(2)}) copy-start(bf16[4,4,32,1024]{3,2,1,0:T(8,128)(2,1)} %get-tuple-element.37) | copy-start | bytes 3145732
  385.9 4.4 %copy-start.1 = (bf16[384,4096]{1,0:T(8,128)(2,1)S(1)}, bf16[384,4096]{1,0:T(8,128)(2,1)}, u32[]{:S(2)}) copy-start(bf16[384,4096]{1,0:T(8,128)(2,1)} %param.17) | copy-start | bytes 9437188

commit v2 on v1

--- a/solution.py
+++ b/solution.py
@@ -80,16 +80,25 @@
                 device_id_type=MESH,
             )
         copy.start()
-        self.open.append((copy, to is None))
-        return copy
-
-    def finish(self, landed=()):
-        for copy, own in self.open:
-            if own:
+        entry = [copy, to is None, False]
+        self.open.append(entry)
+        return entry
+
+    def landed(self, entry):
+        copy, own, seen = entry
+        if not seen:
+            copy.wait() if own else copy.wait_recv()
+            entry[2] = True
+
+    done = landed
+
+    def finish(self):
+        for copy, own, seen in self.open:
+            if own and not seen:
                 copy.wait()
-            elif any(copy is other for other in landed):
+            elif not own and seen:
                 copy.wait_send()
-            else:
+            elif not own:
                 copy.wait()
 
 
@@ -103,9 +112,9 @@
             pl.semaphore_signal(barrier, inc=1, device_id=to, device_id_type=MESH)
         pl.semaphore_wait(barrier, len(peers))
         sender = Sender(refs[-2], refs[-1])
-        landed = body(sender, place, in_refs, out_refs)
+        body(sender, place, in_refs, out_refs)
         assert sender.count == copies, sender.count
-        sender.finish(landed or ())
+        sender.finish()
 
     return pl.pallas_call(
         kernel,
@@ -121,79 +130,274 @@
     )(*ins)
 
 
-def first_body(s, place, ins, outs):
-    xn, go, w = ins
-    xs, gs, wx = outs
+NT = (((1,), (1,)), ((), ()))
+TN = (((0,), (0,)), ((), ()))
+
+
+def front_kernel(
+    lat, go, wq, ch, wi0, wi1, wo, wk, wv, gain, gain2, pick, live,
+    xs_out, wx_out, cap_out, attn_out, gq_out, gkv_out,
+    lat_v, xn_v, wp_v, ch_v, row_v, wi_v, wo_v, wkv_v, wx_v, xs_v, gs_v, gl_v, hid_v,
+    give_v, keep_v, rc_v, fr_v, qs_v, qr_v, q_v, cap_v, kv_v, sel_v, kvr_v,
+    attn_v, gq_v, gkv_v, sems_a, sems_b,
+):
+    place = coords()
     y, zh, zl, x, c = place
-    mine = zl * 2 + c
     pair = core_peer(*place)[0][0]
     across = device(y, zh, 1 - zl, x, c)
-    over = s.send(w, wx.at[span(mine, 256)], across)
-    for to, v in x_peers(*place) + [(None, x)]:
+    here, mine = zl * 4 + x, zl * 2 + c
+    xp = x_peers(*place)
+    chips = []
+    for a in (0, 1):
+        for k in (1, 3, 2, 0):
+            if a or k:
+                chips.append(
+                    (
+                        device(y, zh, (zl + a) % 2, (x + k) % 4, c),
+                        ((zl + a) % 2) * 4 + (x + k) % 4,
+                        ((zl + a) % 2) * 4 + (x + 4 - k) % 4,
+                    )
+                )
+    s = Sender(sems_a, sems_b)
+
+    perm = [
+        s.send(wq.at[:, pl.ds(h * 1024 + v * 256, 256)], wp_v.at[:, pl.ds(v * 512 + h * 256, 256)], None)
+        for h in (0, 1)
+        for v in range(4)
+    ]
+    lat_in = s.send(lat, lat_v, None)
+    ch_in = s.send(ch, ch_v, None)
+    wi_in = [
+        s.send(wi0, wi_v.at[:, pl.ds(0, 384)], None),
+        s.send(wi1, wi_v.at[:, pl.ds(384, 384)], None),
+    ]
+    wo_in = s.send(wo, wo_v, None)
+    wkv_in = [
+        s.send(wk, wkv_v.at[:, pl.ds(0, 128)], None),
+        s.send(wv, wkv_v.at[:, pl.ds(128, 128)], None),
+    ]
+    barrier = pltpu.get_barrier_semaphore()
+    peers = [to for group in (chip_peers, quad_peers) for to, _ in group(*place)]
+    for to in peers:
+        pl.semaphore_signal(barrier, inc=1, device_id=to, device_id_type=MESH)
+    pl.semaphore_wait(barrier, len(peers))
+
+    for copy in perm:
+        s.done(copy)
+    w_over = s.send(wp_v, wx_v.at[span(mine, 256)], across)
+    w_pair = s.send(wp_v, wx_v.at[span(mine, 256)], pair)
+    w_own = s.send(wp_v, wx_v.at[span(mine, 256)], None)
+
+    s.done(lat_in)
+
+    @pl.loop(0, 8)
+    def _(i):
+        rows = pl.ds(pl.multiple_of(i * 16, 16), 16)
+        v = lat_v[rows, :].astype(F32)
+        r = v - jnp.mean(v, axis=-1, keepdims=True)
+        xn_v[rows, :] = (r * lax.rsqrt(jnp.mean(r * r, axis=-1, keepdims=True) + 1e-06)).astype(BF)
+
+    x_in, g_in = [], []
+    for to, v in xp + [(None, x)]:
         for half in (0, 1):
-            s.send(
-                xn.at[:, span(half * 4 + v, 512)],
-                xs.at[span(x, 128), pl.ds(half * 512, 512)],
-                to,
+            x_in.append(
+                s.send(
+                    xn_v.at[:, span(half * 4 + v, 512)],
+                    xs_v.at[span(x, 128), pl.ds(half * 512, 512)],
+                    to,
+                )
             )
-            s.send(
-                go.at[:, span(half * 4 + v, 256)],
-                gs.at[span(x, 128), pl.ds(half * 256, 256)],
-                to,
+    for to, v in xp + [(None, x)]:
+        for half in (0, 1):
+            g_in.append(
+                s.send(
+                    go.at[:, span(half * 4 + v, 256)],
+                    gs_v.at[span(x, 128), pl.ds(half * 256, 256)],
+                    to,
+                )
             )
-    s.send(w, wx.at[span(mine, 256)], pair)
-    s.send(w, wx.at[span(mine, 256)], None)
-    over.wait_recv()
+
+    s.done(ch_in)
+    row_v[...] = ch_v[span(c * 8 + here, 32), :]
+
+    @pl.loop(0, 32)
+    def _(i):
+        rows = pl.ds(pl.multiple_of(i * 16, 16), 16)
+        v = ch_v[rows, :].astype(F32)
+        v = v * lax.rsqrt(jnp.mean(v * v, axis=-1, keepdims=True) + 1e-06) * gain[:1, :].astype(F32)
+        ch_v[rows, :] = v.astype(BF)
+
+    for copy in wi_in:
+        s.done(copy)
+
+    @pl.loop(0, 6)
+    def _(i):
+        rows = pl.ds(pl.multiple_of((i // 3) * 256, 256), 256)
+        cols = pl.ds(pl.multiple_of((i % 3) * 256, 256), 256)
+        gl_v[rows, cols] = jnp.dot(ch_v[rows, :], wi_v[:, cols], preferred_element_type=F32)
+
+    @pl.loop(0, 8)
+    def _(i):
+        rows = pl.ds(pl.multiple_of(i * 64, 64), 64)
+        g, u = gl_v[rows, :384], gl_v[rows, 384:]
+        hid_v[rows, :] = (jax.nn.gelu(g, approximate=True) * u).astype(BF)
+
+    s.done(wo_in)
+
+    def term(which, out):
+        rows = span(which, 256)
+
+        @pl.loop(0, 8)
+        def _(i):
+            cols = pl.ds(pl.multiple_of(i * 512, 512), 512)
+            out[:, cols] = jnp.dot(
+                hid_v[rows, :], wo_v[:, cols], preferred_element_type=F32
+            ).astype(BF)
+
+    term(1 - c, give_v)
+    ff_pair = s.send(give_v, rc_v, pair)
+    term(c, keep_v)
+    s.landed(ff_pair)
+
+    @pl.loop(0, 16)
+    def _(i):
+        rows = pl.ds(pl.multiple_of(i * 16, 16), 16)
+        keep_v[rows, :] = (keep_v[rows, :].astype(F32) + rc_v[rows, :].astype(F32)).astype(BF)
+
+    ff_in = [s.send(keep_v.at[span(j, 32)], fr_v.at[here], to) for to, j, _ in chips]
+    fr_v[here] = keep_v[span(here, 32), :]
+
+    s.landed(w_over)
     theirs = (1 - zl) * 2 + c
-    s.send(wx.at[span(theirs, 256)], wx.at[span(theirs, 256)], pair)
-    return (over,)
+    w_far = s.send(wx_v.at[span(theirs, 256)], wx_v.at[span(theirs, 256)], pair)
+    for copy in x_in + [w_pair, w_own, w_far]:
+        s.landed(copy)
+
+    def query_block(v, out, at):
+        @pl.loop(0, 4)
+        def _(i):
+            rows = pl.ds(pl.multiple_of((i // 2) * 256, 256), 256)
+            cols = pl.ds(pl.multiple_of((i % 2) * 256, 256), 256)
+            from_cols = pl.ds(pl.multiple_of(v * 512 + (i % 2) * 256, 256), 256)
+            out[at, rows, cols] = jnp.dot(
+                xs_v[rows, :], wx_v[:, from_cols], preferred_element_type=F32
+            ).astype(BF)
+
+    q_in = []
+    for k, (to, v) in enumerate(xp):
+        query_block(v, qs_v, k)
+        q_in.append(s.send(qs_v.at[k], qr_v.at[x], to))
+    query_block(x, qr_v, x)
+    s.send(xs_v, xs_out, None)
+    s.send(wx_v, wx_out, None)
+
+    for copy in ff_in:
+        s.landed(copy)
+    ff = fr_v[0].astype(F32)
+    for j in range(1, 8):
+        ff = ff + fr_v[j].astype(F32)
+    r = row_v[...].astype(F32) + ff
+    r = r * lax.rsqrt(jnp.mean(r * r, axis=-1, keepdims=True) + 1e-06) * gain2[:1, :].astype(F32)
+    cap_v[c, here] = r.astype(BF)
+    own = cap_v.at[c, here]
+    cap_in = [(s.send(own, own, to), j) for to, _, j in chips]
+    cap_pair = [s.send(own, own, pair)]
+
+    for copy in q_in:
+        s.landed(copy)
+
+    @pl.loop(0, 8)
+    def _(i):
+        rows = pl.ds(pl.multiple_of(i * 64, 64), 64)
+        q = qr_v[0, rows, :].astype(F32) + qr_v[1, rows, :].astype(F32)
+        q = q + qr_v[2, rows, :].astype(F32) + qr_v[3, rows, :].astype(F32)
+        q_v[rows, :] = q.astype(BF)
+
+    for copy, j in cap_in:
+        s.landed(copy)
+        block = cap_v.at[c, j]
+        cap_pair.append(s.send(block, block, pair))
+    for copy in wkv_in:
+        s.done(copy)
+
+    def key_value(which):
+        rows = cap_v[which].reshape(256, 4096)
+        kv_v[which] = jnp.dot(rows, wkv_v[...], preferred_element_type=F32).astype(BF)
+
+    key_value(c)
+    for copy in cap_pair:
+        s.landed(copy)
+    key_value(1 - c)
+    s.send(cap_v, cap_out, None)
+    for i in (0, 1):
+        p = pick[i, :1, :]
+        both = kv_v[0].astype(F32) * p + kv_v[1].astype(F32) * (1.0 - p)
+        sel_v[i] = both.astype(BF)
+    kv_in = [s.send(sel_v.at[q // 2], kvr_v.at[mine], to) for to, q in quad_peers(*place)]
+    kvr_v[mine] = sel_v[zl]
+    for copy in g_in + kv_in:
+        s.landed(copy)
+
+    inv_root = 1.0 / math.sqrt(HD)
+
+    @pl.loop(0, 4)
+    def _(h):
+        cols = pl.ds(pl.multiple_of(h * HD, HD), HD)
+        q, g = q_v[:, cols], gs_v[:, cols]
+        k, v = kvr_v[h, :, :HD], kvr_v[h, :, HD:]
+        scores = lax.dot_general(q, k, NT, preferred_element_type=F32) * inv_root
+        scores = jnp.where(live[:1, :] > 0.5, scores, -1e30)
+        e = jnp.exp(scores - jnp.max(scores, axis=-1, keepdims=True))
+        probs = e / jnp.sum(e, axis=-1, keepdims=True)
+        probs_b = probs.astype(BF)
+        attn_v[:, cols] = jnp.dot(probs_b, v, preferred_element_type=F32).astype(BF)
+        gp = lax.dot_general(g, v, NT, preferred_element_type=F32)
+        gs = (probs * (gp - jnp.sum(probs * gp, axis=-1, keepdims=True))).astype(BF)
+        gq_v[:, cols] = (jnp.dot(gs, k, preferred_element_type=F32) * inv_root).astype(BF)
+        gk = lax.dot_general(gs, q, TN, preferred_element_type=F32) * inv_root
+        gv = lax.dot_general(probs_b, g, TN, preferred_element_type=F32)
+        gkv_v[h, :, :HD] = gk.astype(BF)
+        gkv_v[h, :, HD:] = gv.astype(BF)
+
+    s.send(attn_v, attn_out, None)
+    s.send(gq_v, gq_out, None)
+    s.send(gkv_v, gkv_out, None)
+    s.finish()
+
+
+FRONT_COPIES = 76
+
+
+def front(*ins):
+    anys, vmem = pl.BlockSpec(memory_space=pl.ANY), pl.BlockSpec(memory_space=pltpu.VMEM)
+    shapes = [(512, 1024), (1024, 2048), (2, 8, 32, 4096), (512, 512), (512, 512), (4, LCAP, 256)]
+    scratch = [
+        (128, 4096), (128, 4096), (256, 2048), (512, 4096), (32, 4096), (4096, 768), (384, 4096),
+        (4096, 256), (1024, 2048), (512, 1024), (512, 512), None, (512, 384),
+        (256, 4096), (256, 4096), (256, 4096), (8, 32, 4096), (3, 512, 512), (4, 512, 512),
+        (512, 512), (2, 8, 32, 4096), (2, LCAP, 256), (2, LCAP, 256), (4, LCAP, 256),
+        (512, 512), (512, 512), (4, LCAP, 256),
+    ]
+    return pl.pallas_call(
+        front_kernel,
+        out_shape=[jax.ShapeDtypeStruct(shape, BF) for shape in shapes],
+        in_specs=[anys] * 9 + [vmem] * 4,
+        out_specs=[anys] * 6,
+        scratch_shapes=[
+            pltpu.VMEM((512, 768), F32) if shape is None else pltpu.VMEM(shape, BF)
+            for shape in scratch
+        ]
+        + [pltpu.SemaphoreType.DMA((FRONT_COPIES,))] * 2,
+        compiler_params=pltpu.CompilerParams(
+            collective_id=0, has_side_effects=True, vmem_limit_bytes=62 * 2**20
+        ),
+        name="front",
+    )(*ins)
 
 
 def core_body(s, place, ins, outs):
     c = place[4]
     s.send(ins[0].at[1 - c], outs[0], core_peer(*place)[0][0])
-
-
-def scatter_body(s, place, ins, outs):
-    ff, qp = ins
-    fr, qr = outs
-    y, zh, zl, x, c = place
-    here = zl * 4 + x
-    for to, j in chip_peers(*place) + [(None, here)]:
-        s.send(ff.at[j], fr.at[here], to)
-    for to, v in x_peers(*place) + [(None, x)]:
-        s.send(qp.at[:, span(v, 512)], qr.at[x], to)
-
-
-def caption_body(s, place, ins, outs):
-    (rows,) = ins
-    (full,) = outs
-    y, zh, zl, x, c = place
-    here = zl * 4 + x
-    pair = core_peer(*place)[0][0]
-    coming = []
-    for a in (0, 1):
-        for k in (1, 3, 2, 0):
-            if a or k:
-                to = device(y, zh, (zl + a) % 2, (x + k) % 4, c)
-                coming.append(
-                    (s.send(rows, full.at[c, here], to), ((zl + a) % 2) * 4 + (x + 4 - k) % 4)
-                )
-    s.send(rows, full.at[c, here], pair)
-    s.send(rows, full.at[c, here], None)
-    for copy, j in coming:
-        copy.wait_recv()
-        s.send(full.at[c, j], full.at[c, j], pair)
-    return tuple(copy for copy, _ in coming)
-
-
-def quad_body(s, place, ins, outs):
-    (sel,) = ins
-    (kv,) = outs
-    y, zh, zl, x, c = place
-    here = zl * 2 + c
-    for to, q in quad_peers(*place) + [(None, here)]:
-        s.send(sel.at[q // 2], kv.at[here], to)
 
 
 def attn_back_body(s, place, ins, outs):
@@ -262,56 +466,6 @@
         s.send(ins[0], outs[0].at[here], to)
 
 
-def attend_kernel(live_ref, q_ref, g_ref, kv_ref, attn_ref, gq_ref, gkv_ref):
-    inv_root = 1.0 / math.sqrt(HD)
-    q, g = q_ref[...], g_ref[...]
-    k, v = kv_ref[0, :, :HD], kv_ref[0, :, HD:]
-    nt = (((1,), (1,)), ((), ()))
-    tn = (((0,), (0,)), ((), ()))
-    scores = lax.dot_general(q, k, nt, preferred_element_type=F32) * inv_root
-    live = lax.broadcasted_iota(jnp.int32, scores.shape, 1) < live_ref[0]
-    scores = jnp.where(live, scores, -1e30)
-    e = jnp.exp(scores - jnp.max(scores, axis=-1, keepdims=True))
-    probs = e / jnp.sum(e, axis=-1, keepdims=True)
-    probs_b = probs.astype(BF)
-    attn_ref[...] = jnp.dot(probs_b, v, preferred_element_type=F32).astype(BF)
-    gp = lax.dot_general(g, v, nt, preferred_element_type=F32)
-    gs = (probs * (gp - jnp.sum(probs * gp, axis=-1, keepdims=True))).astype(BF)
-    gq_ref[...] = (jnp.dot(gs, k, preferred_element_type=F32) * inv_root).astype(BF)
-    gk = lax.dot_general(gs, q, tn, preferred_element_type=F32) * inv_root
-    gv = lax.dot_general(probs_b, g, tn, preferred_element_type=F32)
-    gkv_ref[0, :, :HD] = gk.astype(BF)
-    gkv_ref[0, :, HD:] = gv.astype(BF)
-
-
-def attend(live, q, g, kv):
-    rows = q.shape[0]
-    col = pl.BlockSpec((rows, HD), lambda h: (0, h))
-    per = pl.BlockSpec((1, LCAP, 2 * HD), lambda h: (h, 0, 0))
-    return pl.pallas_call(
-        attend_kernel,
-        grid=(4,),
-        out_shape=[
-            jax.ShapeDtypeStruct(q.shape, BF),
-            jax.ShapeDtypeStruct(q.shape, BF),
-            jax.ShapeDtypeStruct(kv.shape, BF),
-        ],
-        in_specs=[pl.BlockSpec(memory_space=pltpu.SMEM), col, col, per],
-        out_specs=[col, col, per],
-        compiler_params=pltpu.CompilerParams(vmem_limit_bytes=32 * 2**20),
-        name="attend",
-    )(live, q, g, kv)
-
-
-def rms_scale(values, gain):
-    work = values.astype(F32)
-    return (
-        work
-        * lax.rsqrt(jnp.mean(work * work, axis=-1, keepdims=True) + 1e-06)
-        * gain.astype(F32)
-    )
-
-
 def local(
     cap_hidden,
     t5_norm_gain,
@@ -333,71 +487,28 @@
     removed = lat - jnp.mean(lat, axis=-1, keepdims=True)
     rstd = lax.rsqrt(jnp.mean(removed * removed, axis=-1, keepdims=True) + 1e-06)
     xhat = removed * rstd
-    xn = xhat.astype(BF)
-    wq = w_query.reshape(256, 2, 4, 256).transpose(0, 2, 1, 3).reshape(256, 2048)
-    xs, gs, wx = exchange(
-        "tokens_to_features",
-        0,
-        20,
-        first_body,
-        (x_peers, quad_peers),
-        [(512, 1024), (512, 512), (1024, 2048)],
-        xn,
+    pick = jnp.where(caption_of_image == 0, 1.0, 0.0).astype(F32)
+    pick = jnp.broadcast_to(pick[:, None, None], (2, 8, 256))
+    mine = lax.dynamic_index_in_dim(caption_of_image, zl, 0)
+    length = jnp.where(mine == 0, cap_lengths[:1], cap_lengths[1:])
+    live = (jnp.arange(LCAP, dtype=jnp.int32) < length).astype(F32)
+    live = jnp.broadcast_to(live[None], (8, LCAP))
+    xs, wx, caption, attn, gq, gkv = front(
+        latents,
         grad_out,
-        wq,
-    )
-
-    normed = rms_scale(cap_hidden, t5_norm_gain).astype(BF)
-    gate = jnp.dot(normed, t5_wi0, preferred_element_type=F32)
-    lift = jnp.dot(normed, t5_wi1, preferred_element_type=F32)
-    hidden = (jax.nn.gelu(gate, approximate=True) * lift).astype(BF)
-    term = jnp.dot(hidden, t5_wo, preferred_element_type=F32).astype(BF)
-    term = term.reshape(2, 256, 4096)
-    (other,) = exchange(
-        "ff_core_pair", 1, 1, core_body, (core_peer,), [(256, 4096)], term
-    )
-    own = lax.dynamic_index_in_dim(term, c, 0, keepdims=False)
-    ff_pair = (own.astype(F32) + other.astype(F32)).astype(BF)
-    q_part = jnp.dot(xs, wx, preferred_element_type=F32).astype(BF)
-
-    ff_blocks, q_blocks = exchange(
-        "ff_and_query_scatter",
-        2,
-        12,
-        scatter_body,
-        (chip_peers,),
-        [(8, 32, 4096), (4, 512, 512)],
-        ff_pair.reshape(8, 32, 4096),
-        q_part,
-    )
-    ff_rows = jnp.sum(ff_blocks.astype(F32), axis=0)
-    row = c * 256 + (zl * 4 + x) * 32
-    cap_rows = lax.dynamic_slice_in_dim(cap_hidden, row, 32, 0)
-    caption_rows = rms_scale(cap_rows.astype(F32) + ff_rows, t5_final_gain).astype(BF)
-    queries = jnp.sum(q_blocks.astype(F32), axis=0).astype(BF)
-
-    (caption,) = exchange(
-        "caption_gather",
-        3,
-        16,
-        caption_body,
-        (chip_peers, core_peer),
-        [(2, 8, 32, 4096)],
-        caption_rows,
+        w_query,
+        cap_hidden,
+        t5_wi0,
+        t5_wi1,
+        t5_wo,
+        w_key,
+        w_value,
+        jnp.broadcast_to(t5_norm_gain[None], (8, 4096)).astype(F32),
+        jnp.broadcast_to(t5_final_gain[None], (8, 4096)).astype(F32),
+        pick,
+        live,
     )
     caption = caption.reshape(512, 4096)
-    keys = jnp.dot(caption, w_key, preferred_element_type=F32).astype(BF)
-    values = jnp.dot(caption, w_value, preferred_element_type=F32).astype(BF)
-    key_value = jnp.concatenate([keys, values], axis=1).reshape(2, LCAP, 256)
-    chosen = caption_of_image[:, None, None] == 0
-    selected = jnp.where(chosen, key_value[:1], key_value[1:])
-    (kv,) = exchange(
-        "keys_to_heads", 4, 4, quad_body, (quad_peers,), [(4, LCAP, 256)], selected
-    )
-
-    mine = lax.dynamic_index_in_dim(caption_of_image, zl, 0)
-    live = jnp.where(mine == 0, cap_lengths[:1], cap_lengths[1:])
-    attn, gq, gkv = attend(live, queries, gs, kv)
 
     attn_tok, gkv_parts = exchange(
         "attn_to_tokens",

time: 391 us -> 307 us (0.79)
  Pallas kernels: 286 us -> 249 us
  matrix products: 40 us -> 15.1 us
  other arithmetic: 37.8 us -> 23.1 us
  local copies, waits for them, and re-layouts: 23 us -> 16.6 us
    pallas_call x11 -> x6, Pallas kernels: 282 us -> 131 us  [exchange(): pl.pallas_call(kernel, out_shape=[jax.ShapeDtypeStruct(shape, BF) for sha...]
    pallas_call x1, Pallas kernels: 4.34 us -> 118 us  [front(): pl.pallas_call(front_kernel, out_shape=[jax.ShapeDtypeStruct(shape, BF) f...]
    dot_general x5 -> x0, matrix products: 26.5 us -> none  [the longest x1 9.75 us: local(): term = jnp.dot(hidden, t5_wo, preferred_element_type=F32).astype(BF)]
    convert_element_type x5 -> x1, other arithmetic: 8.24 us -> 0.01 us  [local(): live = (jnp.arange(LCAP, dtype=jnp.int32) < length).astype(F32)]
    reduce_sum x4 -> x0, other arithmetic: 6.91 us -> none  [the longest x2 4.3 us: rms_scale(): jnp.mean(work * work, axis=-1, keepdims=True) + 1e-06]
where the time goes in v2:
time: 307 us
  Pallas kernels  249 us (81%)
  other arithmetic  23.1 us (8%)
  local copies, waits for them, and re-layouts  16.6 us (5%)
  matrix products  15.1 us (5%)
    pallas_call x6, Pallas kernels, exchange(): pl.pallas_call(kernel, out_shape=[jax.ShapeDtypeStruct(shape, BF) for sha...  131 us
    pallas_call x1, Pallas kernels, front(): pl.pallas_call(front_kernel, out_shape=[jax.ShapeDtypeStruct(shape, BF) f...  118 us
    convert_element_type x3, local copies, waits for them, and re-layouts, local(): q_full.reshape(256, 4, 2, 256).transpose(0, 2, 1, 3).reshape(256, 2048)  7.39 us
    dot_general x1, matrix products, local(): lax.dot_general(gq_all, wx, (((1,), (1,)), ((), ())), preferred_element_t...  6.3 us

profile of v2, /device:TPU:0, one launch (start us, length us, event | category | flops | bytes accessed | tf_op | source)
XLA Modules:
  0.0 306.5 jit_solution(4612027984787306348)
XLA Ops:
  0.6 0.0 copy-start.10
  0.6 0.0 copy-start.8
  0.7 0.0 copy-start.7
  0.7 0.0 copy-start.6
  0.7 1.2 dynamic_slice.6
  2.6 0.7 broadcast_select_fusion
  3.3 1.5 convert_reduce_fusion.1
  4.7 1.7 fusion.6
  6.4 0.0 copy-done.8
  6.4 0.6 fusion.10
  8.3 0.0 copy-done.10
  8.3 0.6 broadcast_in_dim.61.live
  8.9 0.7 broadcast_in_dim.60.pick
  9.6 0.0 copy-done.6
  9.6 0.7 broadcast_in_dim.56.gain
  10.3 0.0 copy-done.7
  10.3 0.7 broadcast_in_dim.57.gain2
  10.9 117.9 %front.1 = (bf16[512,1024]{1,0:T(8,128)(2,1)}, bf16[1024,2048]{1,0:T(8,128)(2,1)}, bf16[2,8,32,4096]{3,2,1,0:T(8,128)(2,1)}, bf16[512,512]{1,0:T(8,128)(2,1)}, b...) custom-call(bf16[128,4096]{1,0:T(8,128)(2,1)} %lat.1, bf16[128,2048]{1,0:T(8,128)(2,1)} %go.1, ...), custom_call_target="tpu_custom_call" | custom-call | tf_op jit(solution)/shard_map/front/pallas_call | solution.py:381
  128.8 12.9 %attn_to_tokens.1 = (bf16[128,2048]{1,0:T(8,128)(2,1)}, bf16[4,256,256]{2,1,0:T(8,128)(2,1)}) custom-call(bf16[512,512]{1,0:T(8,128)(2,1)} %get-tuple-element.21.refs_0_, bf16[4,256,256]{2,1,0:T(8,128)(2,1)} %get-tuple-element.22.refs_1_), custom_call_target="tpu_custom_call" | custom-call | tf_op jit(solution)/shard_map/attn_to_tokens/pallas_call | solution.py:119
  141.8 2.1 convert_element_type.94
  143.9 1.2 convert_reduce_fusion.2
  145.1 0.1 select_reduce_fusion.1
  145.3 4.8 %convolution_convert_fusion = bf16[4096,256]{1,0:T(8,128)(2,1)} fusion(bf16[512,4096]{1,0:T(8,128)(2,1)} %bitcast.38, bf16[512,256]{1,0:T(8,128)(2,1)S(1)} %bitcast.37), kind=kOutput, calls=%fused_computation | convolution fusion | flops 1074790400 | bytes 6553600 | tf_op jit(solution)/shard_map/dot_general | solution.py:532
  150.1 36.9 %grad_query_gather.1 = (bf16[512,2048]{1,0:T(8,128)(2,1)}, bf16[8,512,256]{2,1,0:T(8,128)(2,1)}) custom-call(bf16[512,512]{1,0:T(8,128)(2,1)} %get-tuple-element.24.refs_0_, bf16[8,512,256]{2,1,0:T(8,128)(2,1)} %bitcast.34), custom_call_target="tpu_custom_call" | custom-call | tf_op jit(solution)/shard_map/grad_query_gather/pallas_call | solution.py:119
  187.0 0.0 copy-start.4
  187.1 6.3 %convolution_convert_fusion.2.refs_0_ = bf16[512,1024]{1,0:T(8,128)(2,1)} fusion(bf16[512,2048]{1,0:T(8,128)(2,1)} %get-tuple-element.27, bf16[1024,2048]{1,0:T(8,128)(2,1)} %get-tuple-element.28), kind=kOutput, calls=%fused_computation.17 | convolution fusion | flops 2148007936 | bytes 7340032 | tf_op jit(solution)/shard_map/dot_general | solution.py:547
  193.4 1.0 reduce_sum.122.refs_2_
  194.4 0.2 copy-done.9
  194.6 4.0 %convolution_convert_fusion.1 = bf16[1024,2048]{1,0:T(8,128)(2,1)S(1)} fusion(bf16[512,1024]{1,0:T(8,128)(2,1)S(1)} %copy-done.9, bf16[512,2048]{1,0:T(8,128)(2,1)} %get-tuple-element.27), kind=kOutput, calls=%fused_computation.3 | convolution fusion | flops 2149580800 | bytes 7340032 | tf_op jit(solution)/shard_map/dot_general | solution.py:550
  198.6 2.2 copy.27
  200.8 4.5 %grad_query_core_pair.1 = bf16[2,256,2048]{2,1,0:T(8,128)(2,1)} custom-call(bf16[2,2,256,2048]{3,2,1,0:T(8,128)(2,1)} %bitcast.30), custom_call_target="tpu_custom_call" | custom-call | tf_op jit(solution)/shard_map/grad_query_core_pair/pallas_call | solution.py:119
  205.3 4.4 %fusion = bf16[2,256,2048]{2,1,0:T(8,128)(2,1)} fusion(bf16[2,256,2048]{2,1,0:T(8,128)(2,1)} %grad_query_core_pair.1, bf16[2,2,256,2048]{3,2,0,1:T(8,128)(2,1)} %copy.27, s32[]{:T(128)S(6)} %select_n.41), kind=kLoop, calls=%fused_computation.2 | loop fusion | flops 4194304 | bytes 6291460 | tf_op jit(solution)/shard_map/convert_element_type | solution.py:558
  209.8 48.7 %grads_scatter.1 = (bf16[128,4096]{1,0:T(8,128)(2,1)}, bf16[4,2,2,32,1024]{4,3,2,1,0:T(8,128)(2,1)}, bf16[4,4,32,1024]{3,2,1,0:T(8,128)(2,1)}, bf16[8,512,256]{2,1,0:T(8,128)(2,1)}) custom-call(bf16[512,1024]{1,0:T(8,128)(2,1)} %convolution_convert_fusion.2.refs_0_, bf16[2,4,2,32,2048]{4,3,2,1,0:T(8,128)(2,1)} %bitcast.31, bf16[512,256]{1,0:T(8,128)(2,1)} %reduce_sum.122.refs_2_), custom_call_target="tpu_custom_call" | custom-call | tf_op jit(solution)/shard_map/grads_scatter/pallas_call | solution.py:119
  258.5 2.3 reduce_sum.125.refs_0_
  260.8 0.0 copy-done
  260.8 2.0 convert_reduce_fusion
  262.8 0.9 reduce_sum.126.refs_1_
  263.7 10.4 %grad_query_scatter.1 = (bf16[4,32,1024]{2,1,0:T(8,128)(2,1)}, bf16[4,32,1024]{2,1,0:T(8,128)(2,1)}) custom-call(bf16[2,2,32,1024]{3,2,1,0:T(8,128)(2,1)} %reduce_sum.125.refs_0_, bf16[4,32,1024]{2,1,0:T(8,128)(2,1)} %reduce_sum.126.refs_1_), custom_call_target="tpu_custom_call" | custom-call | tf_op jit(solution)/shard_map/grad_query_scatter/pallas_call | solution.py:119
  274.1 1.0 reduce.3
  275.1 1.0 reduce.4
  276.1 0.7 pad_maximum_fusion.1.refs_0_
  276.8 17.5 %grad_query_spread.1 = bf16[8,32,2048]{2,1,0:T(8,128)(2,1)} custom-call(bf16[32,2048]{1,0:T(8,128)(2,1)} %pad_maximum_fusion.1.refs_0_), custom_call_target="tpu_custom_call" | custom-call | tf_op jit(solution)/shard_map/grad_query_spread/pallas_call | solution.py:119
  294.3 2.0 fusion.5
  296.3 2.1 reshape.87
  298.5 1.9 copy.24
  300.3 3.4 %reshape.85 = f32[256,2048]{1,0:T(8,128)} reshape(f32[256,2,4,256]{3,2,1,0:T(4,128)} %copy.24) | data formatting | bytes 4194304 | tf_op jit(solution)/shard_map/convert_element_type | solution.py:597
  303.8 0.5 bitcast_convert_fusion
  304.2 2.3 fusion.8
  (17 shorter events, 0.1 us)
Async XLA Ops:
  0.6 7.7 %copy-start.10 = (s32[2]{0:T(128)S(1)}, s32[2]{0:T(128)}, u32[]{:S(2)}) copy-start(s32[2]{0:T(128)} %param.24) | copy-start | bytes 28
  0.6 5.7 %copy-start.8 = (s32[2]{0:T(128)S(1)}, s32[2]{0:T(128)}, u32[]{:S(2)}) copy-start(s32[2]{0:T(128)} %param.19) | copy-start | bytes 28
  0.7 9.6 %copy-start.7 = (bf16[4096]{0:T(1024)(128)(2,1)S(1)}, bf16[4096]{0:T(1024)(128)(2,1)}, u32[]{:S(2)}) copy-start(bf16[4096]{0:T(1024)(128)(2,1)} %param.18) | copy-start | bytes 24580
  0.7 8.9 %copy-start.6 = (bf16[4096]{0:T(1024)(128)(2,1)S(1)}, bf16[4096]{0:T(1024)(128)(2,1)}, u32[]{:S(2)}) copy-start(bf16[4096]{0:T(1024)(128)(2,1)} %param.14) | copy-start | bytes 24580
  187.0 6.3 %copy-start.4 = (bf16[8,512,256]{2,1,0:T(8,128)(2,1)S(1)}, bf16[8,512,256]{2,1,0:T(8,128)(2,1)}, u32[]{:S(2)}) copy-start(bf16[8,512,256]{2,1,0:T(8,128)(2,1)} %get-tuple-element.30) | copy-start | bytes 6291460
  193.4 1.2 copy-start.9
  209.8 51.0 %copy-start = (bf16[128,4096]{1,0:T(8,128)(2,1)S(1)}, bf16[128,4096]{1,0:T(8,128)(2,1)}, u32[]{:S(2)}) copy-start(bf16[128,4096]{1,0:T(8,128)(2,1)} %lat.1) | copy-start | bytes 3145732
  258.5 4.3 %copy-start.5 = (bf16[4,4,32,1024]{3,2,1,0:T(8,128)(2,1)S(1)}, bf16[4,4,32,1024]{3,2,1,0:T(8,128)(2,1)}, u32[]{:S(2)}) copy-start(bf16[4,4,32,1024]{3,2,1,0:T(8,128)(2,1)} %get-tuple-element.33) | copy-start | bytes 3145732
  262.8 31.5 %copy-start.2 = (bf16[128,4096]{1,0:T(8,128)(2,1)S(1)}, bf16[128,4096]{1,0:T(8,128)(2,1)}, u32[]{:S(2)}) copy-start(bf16[128,4096]{1,0:T(8,128)(2,1)} %get-tuple-element.31) | copy-start | bytes 3145732
  294.3 2.0 copy-start.1
  300.3 3.4 %copy-start.3 = (bf16[8,512,256]{2,1,0:T(8,128)(2,1)S(1)}, bf16[8,512,256]{2,1,0:T(8,128)(2,1)}, u32[]{:S(2)}) copy-start(bf16[8,512,256]{2,1,0:T(8,128)(2,1)} %get-tuple-element.36) | copy-start | bytes 6291460

commit v3 on v2

v3 whole, which is shorter than its diff:
```python
import functools
import math

import jax
import jax.numpy as jnp
from jax import lax
from jax.experimental import pallas as pl
from jax.experimental.pallas import tpu as pltpu
from jax.sharding import PartitionSpec as P

HD = 128
LCAP = 256
BF = jnp.bfloat16
F32 = jnp.float32
MESH = pl.DeviceIdType.MESH


def coords():
    d, f = lax.axis_index("dp"), lax.axis_index("fsdp")
    return d // 2, d % 2, f // 8, (f // 2) % 4, f % 2


def device(y, zh, zl, x, c):
    return (y * 2 + zh, zl * 8 + x * 2 + c)


def x_peers(y, zh, zl, x, c):
    return [(device(y, zh, zl, (x + k) % 4, c), (x + k) % 4) for k in (1, 2, 3)]


def y_peers(y, zh, zl, x, c):
    return [(device((y + k) % 4, zh, zl, x, c), (y + k) % 4) for k in (1, 2, 3)]


def z_peers(y, zh, zl, x, c):
    z = zh * 2 + zl
    there = [(z + k) % 4 for k in (1, 2, 3)]
    return [(device(y, t // 2, t % 2, x, c), t) for t in there]


def dp_peers(y, zh, zl, x, c):
    there = [((y + k) % 4, (zh + a) % 2) for a in (0, 1) for k in range(4) if a or k]
    return [(device(v, w, zl, x, c), v * 2 + w) for v, w in there]


def chip_peers(y, zh, zl, x, c):
    there = [((zl + a) % 2, (x + k) % 4) for a in (0, 1) for k in range(4) if a or k]
    return [(device(y, zh, w, v, c), w * 4 + v) for w, v in there]


def quad_peers(y, zh, zl, x, c):
    there = [((zl + a) % 2, (c + b) % 2) for a in (0, 1) for b in (0, 1) if a or b]
    return [(device(y, zh, w, x, b), w * 2 + b) for w, b in there]


def core_peer(y, zh, zl, x, c):
    return [(device(y, zh, zl, x, 1 - c), 1 - c)]


def span(index, size):
    return pl.ds(pl.multiple_of(index * size, size), size)


class Sender:
    def __init__(self, send_sem, recv_sem):
        self.sems, self.count, self.open = (send_sem, recv_sem), 0, []

    def send(self, src, dst, to):
        t = self.count
        self.count += 1
        if to is None:
            copy = pltpu.make_async_copy(src, dst, self.sems[0].at[t])
        else:
            copy = pltpu.make_async_remote_copy(
                src_ref=src,
                dst_ref=dst,
                send_sem=self.sems[0].at[t],
                recv_sem=self.sems[1].at[t],
                device_id=to,
                device_id_type=MESH,
            )
        copy.start()
        entry = [copy, to is None, False]
        self.open.append(entry)
        return entry

    def landed(self, entry):
        copy, own, seen = entry
        if not seen:
            copy.wait() if own else copy.wait_recv()
            entry[2] = True

    done = landed

    def finish(self):
        for copy, own, seen in self.open:
            if own and not seen:
                copy.wait()
            elif not own and seen:
                copy.wait_send()
            elif not own:
                copy.wait()


NT = (((1,), (1,)), ((), ()))
TN = (((0,), (0,)), ((), ()))


def kernel(
    lat, go, wq, ch, wi0, wi1, wo, wk, wv, gain, gain2, flags,
    attn_out, dxn_out, gq_out, gkv_out,
    lat_v, xn_v, wp_v, ch_v, row_v, wi_v, wo_v, wkv_v, wx_v, xs_v, gs_v, gl_v, hid_v,
    give_v, keep_v, rc_v, fr_v, qs_v, qr_v, q_v, cap_v, kv_v, sel_v, kvr_v,
    attn_v, gq_v, gkv_v, gkvr_v, gkvs_v, kvp_v, gqa_v, grc_v, r1_v, r2_v, s1_v, s2_v, t1_v, t2_v,
    fin_v, kvs_v, sems_a, sems_b,
):
    place = coords()
    y, zh, zl, x, c = place
    pair = core_peer(*place)[0][0]
    across = device(y, zh, 1 - zl, x, c)
    here, mine = zl * 4 + x, zl * 2 + c
    xp = x_peers(*place)
    chips = []
    for a in (0, 1):
        for k in (1, 3, 2, 0):
            if a or k:
                chips.append(
                    (
                        device(y, zh, (zl + a) % 2, (x + k) % 4, c),
                        ((zl + a) % 2) * 4 + (x + k) % 4,
                        ((zl + a) % 2) * 4 + (x + 4 - k) % 4,
                    )
                )
    s = Sender(sems_a, sems_b)

    perm = [
        s.send(wq.at[:, pl.ds(h * 1024 + v * 256, 256)], wp_v.at[:, pl.ds(v * 512 + h * 256, 256)], None)
        for h in (0, 1)
        for v in range(4)
    ]
    lat_in = s.send(lat, lat_v, None)
    ch_in = [s.send(ch.at[pl.ds(i * 128, 128)], ch_v.at[i], None) for i in range(4)]
    wi_in = [
        s.send(wi0, wi_v.at[:, pl.ds(0, 384)], None),
        s.send(wi1, wi_v.at[:, pl.ds(384, 384)], None),
    ]
    wo_in = s.send(wo, wo_v, None)
    wkv_in = [
        s.send(wk, wkv_v.at[:, pl.ds(0, 128)], None),
        s.send(wv, wkv_v.at[:, pl.ds(128, 128)], None),
    ]
    barrier = pltpu.get_barrier_semaphore()
    peers = [to for group in GROUPS for to, _ in group(*place)]
    for to in peers:
        pl.semaphore_signal(barrier, inc=1, device_id=to, device_id_type=MESH)
    pl.semaphore_wait(barrier, len(peers))

    for copy in perm:
        s.done(copy)
    w_over = s.send(wp_v, wx_v.at[span(mine, 256)], across)
    w_pair = s.send(wp_v, wx_v.at[span(mine, 256)], pair)
    w_own = s.send(wp_v, wx_v.at[span(mine, 256)], None)

    s.done(lat_in)

    @pl.loop(0, 8)
    def _(i):
        rows = pl.ds(pl.multiple_of(i * 16, 16), 16)
        v = lat_v[rows, :].astype(F32)
        r = v - jnp.mean(v, axis=-1, keepdims=True)
        xn_v[rows, :] = (r * lax.rsqrt(jnp.mean(r * r, axis=-1, keepdims=True) + 1e-06)).astype(BF)

    x_in, g_in = [], []
    for to, v in xp + [(None, x)]:
        for half in (0, 1):
            x_in.append(
                s.send(
                    xn_v.at[:, span(half * 4 + v, 512)],
                    xs_v.at[span(x, 128), pl.ds(half * 512, 512)],
                    to,
                )
            )
    for to, v in xp + [(None, x)]:
        for half in (0, 1):
            g_in.append(
                s.send(
                    go.at[:, span(half * 4 + v, 256)],
                    gs_v.at[span(x, 128), pl.ds(half * 256, 256)],
                    to,
                )
            )

    for copy in ch_in:
        s.done(copy)
    row_v[...] = ch_v[c * 2 + here // 4, span(here % 4, 32), :]

    @pl.loop(0, 32)
    def _(i):
        rows = pl.ds(pl.multiple_of((i % 8) * 16, 16), 16)
        v = ch_v[i // 8, rows, :].astype(F32)
        v = v * lax.rsqrt(jnp.mean(v * v, axis=-1, keepdims=True) + 1e-06) * gain[...].astype(F32)
        ch_v[i // 8, rows, :] = v.astype(BF)

    for copy in wi_in:
        s.done(copy)

    @pl.loop(0, 6)
    def _(i):
        rows = pl.ds(pl.multiple_of((i // 3) * 256, 256), 256)
        cols = pl.ds(pl.multiple_of((i % 3) * 256, 256), 256)
        normed = ch_v[pl.ds((i // 3) * 2, 2)].reshape(256, 4096)
        gl_v[rows, cols] = jnp.dot(normed, wi_v[:, cols], preferred_element_type=F32)

    @pl.loop(0, 8)
    def _(i):
        rows = pl.ds(pl.multiple_of(i * 64, 64), 64)
        g, u = gl_v[rows, :384], gl_v[rows, 384:]
        hid_v[rows, :] = (jax.nn.gelu(g, approximate=True) * u).astype(BF)

    s.done(wo_in)

    def term(which, out):
        rows = span(which, 256)

        @pl.loop(0, 8)
        def _(i):
            cols = pl.ds(pl.multiple_of(i * 512, 512), 512)
            out[:, cols] = jnp.dot(
                hid_v[rows, :], wo_v[:, cols], preferred_element_type=F32
            ).astype(BF)

    term(1 - c, give_v)
    ff_pair = s.send(give_v, rc_v, pair)
    term(c, keep_v)
    s.landed(ff_pair)

    @pl.loop(0, 16)
    def _(i):
        rows = pl.ds(pl.multiple_of(i * 16, 16), 16)
        keep_v[rows, :] = (keep_v[rows, :].astype(F32) + rc_v[rows, :].astype(F32)).astype(BF)

    ff_in = [s.send(keep_v.at[span(j, 32)], fr_v.at[here], to) for to, j, _ in chips]
    fr_v[here] = keep_v[span(here, 32), :]

    s.landed(w_over)
    theirs = (1 - zl) * 2 + c
    w_far = s.send(wx_v.at[span(theirs, 256)], wx_v.at[span(theirs, 256)], pair)
    for copy in x_in + [w_pair, w_own, w_far]:
        s.landed(copy)

    def query_block(v, out, at):
        @pl.loop(0, 4)
        def _(i):
            rows = pl.ds(pl.multiple_of((i // 2) * 256, 256), 256)
            cols = pl.ds(pl.multiple_of((i % 2) * 256, 256), 256)
            from_cols = pl.ds(pl.multiple_of(v * 512 + (i % 2) * 256, 256), 256)
            out[at, rows, cols] = jnp.dot(
                xs_v[rows, :], wx_v[:, from_cols], preferred_element_type=F32
            ).astype(BF)

    q_in = []
    for k, (to, v) in enumerate(xp):
        query_block(v, qs_v, k)
        q_in.append(s.send(qs_v.at[k], qr_v.at[x], to))
    query_block(x, qr_v, x)

    for copy in ff_in:
        s.landed(copy)
    ff = fr_v[0].astype(F32)
    for j in range(1, 8):
        ff = ff + fr_v[j].astype(F32)
    r = row_v[...].astype(F32) + ff
    r = r * lax.rsqrt(jnp.mean(r * r, axis=-1, keepdims=True) + 1e-06) * gain2[...].astype(F32)
    cap_v[c, here] = r.astype(BF)
    own = cap_v.at[c, here]
    cap_in = [(s.send(own, own, to), j) for to, _, j in chips]
    cap_pair = [s.send(own, own, pair)]

    for copy in q_in:
        s.landed(copy)

    @pl.loop(0, 8)
    def _(i):
        rows = pl.ds(pl.multiple_of(i * 64, 64), 64)
        q = qr_v[0, rows, :].astype(F32) + qr_v[1, rows, :].astype(F32)
        q = q + qr_v[2, rows, :].astype(F32) + qr_v[3, rows, :].astype(F32)
        q_v[rows, :] = q.astype(BF)

    for copy, j in cap_in:
        s.landed(copy)
        block = cap_v.at[c, j]
        cap_pair.append(s.send(block, block, pair))
    for copy in wkv_in:
        s.done(copy)

    def key_value(which):
        rows = cap_v[which].reshape(256, 4096)
        kv_v[which] = jnp.dot(rows, wkv_v[...], preferred_element_type=F32).astype(BF)

    key_value(c)
    for copy in cap_pair:
        s.landed(copy)
    key_value(1 - c)
    for i in (0, 1):
        p = flags[i : i + 1, :]
        both = kv_v[0].astype(F32) * p + kv_v[1].astype(F32) * (1.0 - p)
        sel_v[i] = both.astype(BF)
    kv_in = [s.send(sel_v.at[q // 2], kvr_v.at[mine], to) for to, q in quad_peers(*place)]
    kvr_v[mine] = sel_v[zl]
    for copy in g_in + kv_in:
        s.landed(copy)

    inv_root = 1.0 / math.sqrt(HD)

    @pl.loop(0, 4)
    def _(h):
        cols = pl.ds(pl.multiple_of(h * HD, HD), HD)
        q, g = q_v[:, cols], gs_v[:, cols]
        k, v = kvr_v[h, :, :HD], kvr_v[h, :, HD:]
        scores = lax.dot_general(q, k, NT, preferred_element_type=F32) * inv_root
        scores = jnp.where(flags[2:3, :] > 0.5, scores, -1e30)
        e = jnp.exp(scores - jnp.max(scores, axis=-1, keepdims=True))
        probs = e / jnp.sum(e, axis=-1, keepdims=True)
        probs_b = probs.astype(BF)
        attn_v[:, cols] = jnp.dot(probs_b, v, preferred_element_type=F32).astype(BF)
        gp = lax.dot_general(g, v, NT, preferred_element_type=F32)
        gs = (probs * (gp - jnp.sum(probs * gp, axis=-1, keepdims=True))).astype(BF)
        gq_v[:, cols] = (jnp.dot(gs, k, preferred_element_type=F32) * inv_root).astype(BF)
        gk = lax.dot_general(gs, q, TN, preferred_element_type=F32) * inv_root
        gv = lax.dot_general(probs_b, g, TN, preferred_element_type=F32)
        gkv_v[h, :, :HD] = gk.astype(BF)
        gkv_v[h, :, HD:] = gv.astype(BF)

    gq_in = [s.send(gq_v, gqa_v.at[:, span(x, 512)], to) for to, _ in xp]
    gq_in.append(s.send(gq_v, gqa_v.at[:, span(x, 512)], None))
    gkv_in = [
        s.send(gkv_v.at[q], gkvr_v.at[mine], to) for to, q in quad_peers(*place)
    ]
    gkvr_v[mine] = gkv_v[mine]
    for to, v in xp + [(None, x)]:
        for half in (0, 1):
            s.send(
                attn_v.at[span(v, 128), pl.ds(half * 256, 256)],
                attn_out.at[:, span(half * 4 + x, 256)],
                to,
            )
    for copy in gkv_in:
        s.landed(copy)
    im0 = gkvr_v[0].astype(F32) + gkvr_v[1].astype(F32)
    im1 = gkvr_v[2].astype(F32) + gkvr_v[3].astype(F32)
    p0, p1 = flags[0:1, :], flags[1:2, :]
    gkvs_v[:LCAP, :] = (im0 * p0 + im1 * p1).astype(BF)
    gkvs_v[LCAP:, :] = (im0 * (1.0 - p0) + im1 * (1.0 - p1)).astype(BF)

    def kv_block(j):
        cols = span(j, 512)
        rows = cap_v[:, :, :, cols].reshape(512, 512)
        kvp_v[j] = lax.dot_general(rows, gkvs_v[...], TN, preferred_element_type=F32).astype(BF)

    kv_sum_in = []
    here_dp = y * 2 + zh
    for k, (to, j) in enumerate(dp_peers(*place)):
        kv_block(j)
        kv_sum_in.append(s.send(kvp_v.at[j], kvs_v.at[k], to))
    kv_block(here_dp)

    for copy in gq_in:
        s.landed(copy)

    def q_grad(which, at):
        @pl.loop(0, 8)
        def _(i):
            f = i // 4
            cols = pl.ds(pl.multiple_of((i % 4) * 512, 512), 512)
            to_cols = pl.ds(pl.multiple_of(at + (i % 4) * 512, 512), 512)
            from_rows = pl.ds(pl.multiple_of(f * 512 + which * 256, 256), 256)
            part = lax.dot_general(
                xs_v[:, from_rows], gqa_v[:, cols], TN, preferred_element_type=F32
            ).astype(BF)
            ch_v[f * 2, :, to_cols] = part[:128]
            ch_v[f * 2 + 1, :, to_cols] = part[128:]

    q_grad(1 - c, 0)
    qg_pair = s.send(ch_v.at[:, :, pl.ds(0, 2048)], grc_v, pair)
    q_grad(c, 2048)

    @pl.loop(0, 4)
    def _(i):
        rows = pl.ds(pl.multiple_of(i * 256, 256), 256)
        part = lax.dot_general(
            gqa_v[...], wx_v[rows, :], NT, preferred_element_type=F32
        ).astype(BF)
        for v in range(4):
            lat_v[:, pl.ds(pl.multiple_of(v * 1024 + i * 256, 256), 256)] = part[
                v * 128 : (v + 1) * 128
            ]

    for to, v in xp + [(None, x)]:
        for half in (0, 1):
            s.send(
                lat_v.at[:, span(v * 2 + half, 512)],
                dxn_out.at[:, span(half * 4 + x, 512)],
                to,
            )
    s.landed(qg_pair)

    @pl.loop(0, 32)
    def _(i):
        rows = pl.ds(pl.multiple_of((i % 8) * 16, 16), 16)
        keep = ch_v[i // 8, rows, 2048:].astype(F32) + grc_v[i // 8, rows, :].astype(F32)
        ch_v[i // 8, rows, 2048:] = keep.astype(BF)

    yp, zp = y_peers(*place), z_peers(*place)
    r1_in = [
        s.send(ch_v.at[:, span(v, 32), pl.ds(2048, 1024)], r1_v.at[k], to)
        for k, (to, v) in enumerate(yp)
    ]
    r2_in = [
        s.send(ch_v.at[(t % 2) * 2 + t // 2, :, pl.ds(3072, 1024)], r2_v.at[k], to)
        for k, (to, t) in enumerate(zp)
    ]

    for copy in kv_sum_in:
        s.landed(copy)

    @pl.loop(0, 8)
    def _(i):
        rows = pl.ds(pl.multiple_of(i * 64, 64), 64)
        total = kvp_v[here_dp, rows, :].astype(F32)
        for k in range(7):
            total = total + kvs_v[k, rows, :].astype(F32)
        kvp_v[here_dp, rows, :] = total.astype(BF)

    for to, _ in dp_peers(*place) + [(None, 0)]:
        s.send(kvp_v.at[here_dp], gkv_out.at[here_dp], to)

    for copy in r1_in + r2_in:
        s.landed(copy)
    for i in range(4):
        total = ch_v[i, span(y, 32), 2048:3072].astype(F32)
        for k in range(3):
            total = total + r1_v[k, i].astype(F32)
        s1_v[i] = total.astype(BF)
    at = zl * 2 + zh
    for i in range(4):
        rows = pl.ds(i * 32, 32)
        total = ch_v[at, rows, 3072:].astype(F32)
        for k in range(3):
            total = total + r2_v[k, rows, :].astype(F32)
        s2_v[i] = total.astype(BF)
    t_in = [
        s.send(s1_v.at[(t % 2) * 2 + t // 2], t1_v.at[k], to) for k, (to, t) in enumerate(zp)
    ]
    t_in += [s.send(s2_v.at[v], t2_v.at[k], to) for k, (to, v) in enumerate(yp)]
    for copy in t_in:
        s.landed(copy)
    left, right = s1_v[at].astype(F32), s2_v[y].astype(F32)
    for k in range(3):
        left = left + t1_v[k].astype(F32)
        right = right + t2_v[k].astype(F32)
    fin_v[:, :1024] = left.astype(BF)
    fin_v[:, 1024:] = right.astype(BF)
    for to, _ in dp_peers(*place) + [(None, 0)]:
        s.send(fin_v, gq_out.at[zh * 4 + y], to)
    s.finish()


GROUPS = (chip_peers, quad_peers, dp_peers, z_peers)
COPIES = 150


def main(*ins):
    anys, vmem = pl.BlockSpec(memory_space=pl.ANY), pl.BlockSpec(memory_space=pltpu.VMEM)
    shapes = [(128, 2048), (128, 4096), (8, 32, 2048), (8, 512, 256)]
    scratch = [
        (128, 4096), (128, 4096), (256, 2048), (4, 128, 4096), (32, 4096), (4096, 768), (384, 4096),
        (4096, 256), (1024, 2048), (512, 1024), (512, 512), None, (512, 384),
        (256, 4096), (256, 4096), (256, 4096), (8, 32, 4096), (3, 512, 512), (4, 512, 512),
        (512, 512), (2, 8, 32, 4096), (2, LCAP, 256), (2, LCAP, 256), (4, LCAP, 256),
        (512, 512), (512, 512), (4, LCAP, 256), (4, LCAP, 256), (512, 256), (8, 512, 256),
        (512, 2048), (4, 128, 2048), (3, 4, 32, 1024), (3, 128, 1024), (4, 32, 1024), (4, 32, 1024),
        (3, 32, 1024), (3, 32, 1024), (32, 2048), (7, 512, 256),
    ]
    return pl.pallas_call(
        kernel,
        out_shape=[jax.ShapeDtypeStruct(shape, BF) for shape in shapes],
        in_specs=[anys] * 9 + [vmem] * 3,
        out_specs=[anys] * 4,
        scratch_shapes=[
            pltpu.VMEM((512, 768), F32) if shape is None else pltpu.VMEM(shape, BF)
            for shape in scratch
        ]
        + [pltpu.SemaphoreType.DMA((COPIES,))] * 2,
        compiler_params=pltpu.CompilerParams(
            collective_id=0, has_side_effects=True, vmem_limit_bytes=63 * 2**20
        ),
        name="main",
    )(*ins)


def last_kernel(attn, dxn, lat, gq, gkv, attn_o, lat_o, gq_o, gk_o, gv_o):
    attn_o[...] = attn[...].astype(F32)
    v = lat[...].astype(F32)
    r = v - jnp.mean(v, axis=-1, keepdims=True)
    rstd = lax.rsqrt(jnp.mean(r * r, axis=-1, keepdims=True) + 1e-06)
    xhat = r * rstd
    g = dxn[...].astype(F32)
    lat_o[...] = rstd * (
        g
        - jnp.mean(g, axis=-1, keepdims=True)
        - xhat * jnp.mean(g * xhat, axis=-1, keepdims=True)
    )
    for w in range(4):
        for h in (0, 1):
            there, here = h * 1024 + w * 256, w * 512 + h * 256
            gq_o[:, there : there + 256] = gq[0, :, here : here + 256].astype(F32)
    gk_o[...] = gkv[0, :, :HD].astype(F32)
    gv_o[...] = gkv[0, :, HD:].astype(F32)


def last(attn, dxn, lat, gq, gkv):
    def rows(count, width):
        return pl.BlockSpec((count, width), lambda i: (i, 0))

    return pl.pallas_call(
        last_kernel,
        grid=(8,),
        out_shape=[
            jax.ShapeDtypeStruct(shape, F32)
            for shape in [(128, 2048), (128, 4096), (256, 2048), (4096, HD), (4096, HD)]
        ],
        in_specs=[
            rows(16, 2048),
            rows(16, 4096),
            rows(16, 4096),
            pl.BlockSpec((1, 32, 2048), lambda i: (i, 0, 0)),
            pl.BlockSpec((1, 512, 256), lambda i: (i, 0, 0)),
        ],
        out_specs=[
            rows(16, 2048),
            rows(16, 4096),
            rows(32, 2048),
            rows(512, HD),
            rows(512, HD),
        ],
        compiler_params=pltpu.CompilerParams(vmem_limit_bytes=32 * 2**20),
        name="last",
    )(attn, dxn, lat, gq, gkv)


def local(
    cap_hidden,
    t5_norm_gain,
    t5_wi0,
    t5_wi1,
    t5_wo,
    t5_final_gain,
    cap_lengths,
    latents,
    w_query,
    w_key,
    w_value,
    caption_of_image,
    grad_out,
):
    zl = lax.axis_index("fsdp") // 8
    first = (caption_of_image == 0).astype(F32)
    mine = lax.dynamic_index_in_dim(caption_of_image, zl, 0)
    length = jnp.where(mine == 0, cap_lengths[:1], cap_lengths[1:])
    live = (jnp.arange(LCAP, dtype=jnp.int32) < length).astype(F32)
    flags = jnp.concatenate([jnp.broadcast_to(first[:, None], (2, LCAP)), live[None]])
    attn, dxn, gq, gkv = main(
        latents,
        grad_out,
        w_query,
        cap_hidden,
        t5_wi0,
        t5_wi1,
        t5_wo,
        w_key,
        w_value,
        t5_norm_gain[None],
        t5_final_gain[None],
        flags,
    )
    return last(attn, dxn, latents, gq, gkv)


def solution(mesh):
    placed = (
        P("dp", None),
        P(),
        P(None, "fsdp"),
        P(None, "fsdp"),
        P("fsdp", None),
        P(),
        P("dp"),
        P(("dp", "fsdp"), None),
        P("fsdp", None),
        P(None, "fsdp"),
        P(None, "fsdp"),
        P("dp"),
        P(("dp", "fsdp"), None),
    )
    return jax.shard_map(
        local,
        mesh=mesh,
        in_specs=placed,
        out_specs=(
            P(("dp", "fsdp"), None),
            P(("dp", "fsdp"), None),
            P("fsdp", None),
            P(None, "fsdp"),
            P(None, "fsdp"),
        ),
        check_vma=False,
    )
```

time: 307 us -> 249 us (0.81)
  the two profiles are of different devices: /device:TPU:0 before, /device:TPU:2 now
where the time goes in v3:
time: 249 us; the launch traced here: 248 us
  Pallas kernels  233 us (94%)
  local copies, waits for them, and re-layouts  11.5 us (5%)
  between operations  2.63 us (1%)
    pallas_call x1, Pallas kernels, main(): pl.pallas_call(kernel, out_shape=[jax.ShapeDtypeStruct(shape, BF) for sha...  227 us
    unnamed x10, local copies, waits for them, and re-layouts  6.3 us
    pallas_call x1, Pallas kernels, last(): pl.pallas_call(last_kernel, grid=(8,), out_shape=[jax.ShapeDtypeStruct(sh...  5.54 us

profile of v3, /device:TPU:2, one launch (start us, length us, event | category | flops | bytes accessed | tf_op | source)
XLA Modules:
  0.0 248.4 jit_solution(17565941895806137446)
XLA Ops:
  0.6 1.2 dynamic_slice.4
  2.5 0.7 compare_convert_fusion.1
  3.2 1.3 fusion
  5.8 0.7 pad_maximum_fusion.flags
  6.5 1.3 broadcast_in_dim.6.gain
  7.8 1.3 broadcast_in_dim.14.gain2
  9.1 227.4 %main.1 = (bf16[128,2048]{1,0:T(8,128)(2,1)}, bf16[128,4096]{1,0:T(8,128)(2,1)}, bf16[8,32,2048]{2,1,0:T(8,128)(2,1)}, bf16[8,512,256]{2,1,0:T(8,128)(2,1)}) custom-call(bf16[128,4096]{1,0:T(8,128)(2,1)} %lat.3, bf16[128,2048]{1,0:T(8,128)(2,1)} %go.1, bf16[256,2048]{1,0:T(8,128)(2,1)} %wq.1, bf16[512,4096]{1,0:T(8,128)(2,1)} %ch.1, bf16[4096,384]{1,0:T(8,128)(2,1)} %wi0.1, ...), custom_call_target="tpu_custom_call" | custom-call | tf_op jit(solution)/shard_map/main/pallas_call | solution.py:484
  236.5 0.0 copy-start
  236.5 1.2 copy-done
  237.7 0.0 copy-start.1
  237.7 1.6 copy-done.1
  239.3 0.0 copy-start.2
  239.3 1.2 copy-done.2
  240.6 0.0 copy-start.3
  240.6 1.2 copy-done.3
  241.8 0.0 copy-start.4
  241.8 1.0 copy-done.4
  242.8 5.5 %last.1 = (f32[128,2048]{1,0:T(8,128)}, f32[128,4096]{1,0:T(8,128)}, f32[256,2048]{1,0:T(8,128)}, f32[4096,128]{1,0:T(8,128)}, f32[4096,128]{1,0:T(8,128)}) custom-call(bf16[128,2048]{1,0:T(8,128)(2,1)S(1)} %copy-done.4, bf16[128,4096]{1,0:T(8,128)(2,1)S(1)} %copy-done.2, bf16[128,4096]{1,0:T(8,128)(2,1)S(1)} %copy-done, bf16[8,32,2048]{2,1,0:T(8,128)(2,1)S(1)} %copy-done.3, ...), custom_call_target="tpu_custom_call" | custom-call | tf_op jit(solution)/shard_map/last/pallas_call | solution.py:525
  (2 shorter events, 0.0 us)
Async XLA Ops:
  236.5 1.2 copy-start
  237.7 1.6 copy-start.1
  239.3 1.2 copy-start.2
  240.6 1.2 copy-start.3
  241.8 1.0 copy-start.4

commit v4 on v3

--- a/solution.py
+++ b/solution.py
@@ -107,10 +107,10 @@
 
 
 def kernel(
-    lat, go, wq, ch, wi0, wi1, wo, wk, wv, gain, gain2, flags,
+    lat, go, wq, ch, wi0, wi1, wo, wk, wv, gain, gain2, lengths, owner,
     attn_out, dxn_out, gq_out, gkv_out,
     lat_v, xn_v, wp_v, ch_v, row_v, wi_v, wo_v, wkv_v, wx_v, xs_v, gs_v, gl_v, hid_v,
-    give_v, keep_v, rc_v, fr_v, qs_v, qr_v, q_v, cap_v, kv_v, sel_v, kvr_v,
+    give_v, keep_v, rc_v, fz_v, fr_v, qs_v, qr_v, q_v, cap_v, kv_v, sel_v, kvr_v,
     attn_v, gq_v, gkv_v, gkvr_v, gkvs_v, kvp_v, gqa_v, grc_v, r1_v, r2_v, s1_v, s2_v, t1_v, t2_v,
     fin_v, kvs_v, sems_a, sems_b,
 ):
@@ -118,20 +118,13 @@
     y, zh, zl, x, c = place
     pair = core_peer(*place)[0][0]
     across = device(y, zh, 1 - zl, x, c)
+    behind = device(y, 1 - zh, 1 - zl, x, c)
     here, mine = zl * 4 + x, zl * 2 + c
     xp = x_peers(*place)
-    chips = []
-    for a in (0, 1):
-        for k in (1, 3, 2, 0):
-            if a or k:
-                chips.append(
-                    (
-                        device(y, zh, (zl + a) % 2, (x + k) % 4, c),
-                        ((zl + a) % 2) * 4 + (x + k) % 4,
-                        ((zl + a) % 2) * 4 + (x + 4 - k) % 4,
-                    )
-                )
     s = Sender(sems_a, sems_b)
+    one = [1.0 - jnp.minimum(owner[i], 1).astype(F32) for i in (0, 1)]
+    mine_first = 1 - jnp.minimum(owner[zl], 1)
+    length = lengths[0] * mine_first + lengths[1] * (1 - mine_first)
 
     perm = [
         s.send(wq.at[:, pl.ds(h * 1024 + v * 256, 256)], wp_v.at[:, pl.ds(v * 512 + h * 256, 256)], None)
@@ -157,7 +150,10 @@
 
     for copy in perm:
         s.done(copy)
-    w_over = s.send(wp_v, wx_v.at[span(mine, 256)], across)
+    w_over = [
+        s.send(wp_v.at[pl.ds(i * 128, 128)], wx_v.at[span(mine * 2 + i, 128)], to)
+        for i, to in enumerate((across, behind))
+    ]
     w_pair = s.send(wp_v, wx_v.at[span(mine, 256)], pair)
     w_own = s.send(wp_v, wx_v.at[span(mine, 256)], None)
 
@@ -194,11 +190,13 @@
         s.done(copy)
     row_v[...] = ch_v[c * 2 + here // 4, span(here % 4, 32), :]
 
+    gain_row = gain[...].astype(F32).reshape(1, 4096)
+
     @pl.loop(0, 32)
     def _(i):
         rows = pl.ds(pl.multiple_of((i % 8) * 16, 16), 16)
         v = ch_v[i // 8, rows, :].astype(F32)
-        v = v * lax.rsqrt(jnp.mean(v * v, axis=-1, keepdims=True) + 1e-06) * gain[...].astype(F32)
+        v = v * lax.rsqrt(jnp.mean(v * v, axis=-1, keepdims=True) + 1e-06) * gain_row
         ch_v[i // 8, rows, :] = v.astype(BF)
 
     for copy in wi_in:
@@ -234,15 +232,23 @@
     term(c, keep_v)
     s.landed(ff_pair)
 
-    @pl.loop(0, 16)
-    def _(i):
-        rows = pl.ds(pl.multiple_of(i * 16, 16), 16)
-        keep_v[rows, :] = (keep_v[rows, :].astype(F32) + rc_v[rows, :].astype(F32)).astype(BF)
-
-    ff_in = [s.send(keep_v.at[span(j, 32)], fr_v.at[here], to) for to, j, _ in chips]
-    fr_v[here] = keep_v[span(here, 32), :]
-
-    s.landed(w_over)
+    def add_core(z):
+        @pl.loop(0, 8)
+        def _(i):
+            rows = pl.ds(pl.multiple_of(z * 128 + i * 16, 16), 16)
+            total = keep_v[rows, :].astype(F32) + rc_v[rows, :].astype(F32)
+            keep_v[rows, :] = total.astype(BF)
+
+    add_core(1 - zl)
+    order = [1, 3, 2, 0]
+    fz_in = [
+        s.send(keep_v.at[span((1 - zl) * 4 + (x + k) % 4, 32)], fz_v.at[(x + k) % 4], across)
+        for k in order
+    ]
+    add_core(zl)
+
+    for copy in w_over:
+        s.landed(copy)
     theirs = (1 - zl) * 2 + c
     w_far = s.send(wx_v.at[span(theirs, 256)], wx_v.at[span(theirs, 256)], pair)
     for copy in x_in + [w_pair, w_own, w_far]:
@@ -259,23 +265,65 @@
             ).astype(BF)
 
     q_in = []
-    for k, (to, v) in enumerate(xp):
-        query_block(v, qs_v, k)
-        q_in.append(s.send(qs_v.at[k], qr_v.at[x], to))
+    for k in (0, 2):
+        query_block(xp[k][1], qs_v, k)
+        q_in.append(s.send(qs_v.at[k], qr_v.at[x], xp[k][0]))
+
+    ff_in = []
+
+    def add_across(n):
+        k = order[n]
+        s.landed(fz_in[n])
+        v = (x + k) % 4
+        rows = span(zl * 4 + v, 32)
+        total = keep_v[rows, :].astype(F32) + fz_v[v].astype(F32)
+        if k:
+            keep_v[rows, :] = total.astype(BF)
+            ff_in.append(s.send(keep_v.at[rows], fr_v.at[k - 1], xp[k - 1][0]))
+        return total
+
+    add_across(0)
+    query_block(xp[1][1], qs_v, 1)
+    add_across(1)
     query_block(x, qr_v, x)
+    add_across(2)
+    ff = add_across(3)
+    q_in.append(s.send(qs_v.at[1], qr_v.at[x], xp[1][0]))
 
     for copy in ff_in:
         s.landed(copy)
-    ff = fr_v[0].astype(F32)
-    for j in range(1, 8):
-        ff = ff + fr_v[j].astype(F32)
+    for k in range(3):
+        ff = ff + fr_v[k].astype(F32)
     r = row_v[...].astype(F32) + ff
-    r = r * lax.rsqrt(jnp.mean(r * r, axis=-1, keepdims=True) + 1e-06) * gain2[...].astype(F32)
+    r = r * lax.rsqrt(jnp.mean(r * r, axis=-1, keepdims=True) + 1e-06) * gain2[...].astype(F32).reshape(1, 4096)
     cap_v[c, here] = r.astype(BF)
     own = cap_v.at[c, here]
-    cap_in = [(s.send(own, own, to), j) for to, _, j in chips]
-    cap_pair = [s.send(own, own, pair)]
-
+    there = (1 - zl) * 4 + x
+
+    def piece(j, half):
+        return cap_v.at[c, j, pl.ds(half * 16, 16)]
+
+    def pass_on(ref, to):
+        return s.send(ref, ref, to)
+
+    z_own = [pass_on(piece(here, half), across) for half in (0, 1)]
+    x_own = [(k, pass_on(own, xp[k - 1][0])) for k in (1, 3, 2)]
+    cap_pair = [pass_on(own, pair)]
+    s.landed(z_own[0])
+    x_far = [(k, pass_on(piece(there, 0), xp[k - 1][0])) for k in (1, 3, 2)]
+    cap_pair.append(pass_on(piece(there, 0), pair))
+    z_far = []
+    for k, copy in x_own:
+        s.landed(copy)
+        j = zl * 4 + (x + 4 - k) % 4
+        z_far.append((k, pass_on(piece(j, 1), across)))
+        cap_pair.append(pass_on(cap_v.at[c, j], pair))
+    s.landed(z_own[1])
+    cap_pair.append(pass_on(piece(there, 1), pair))
+    for half, group in ((0, x_far), (1, z_far)):
+        for k, copy in group:
+            s.landed(copy)
+            cap_pair.append(pass_on(piece((1 - zl) * 4 + (x + 4 - k) % 4, half), pair))
     for copy in q_in:
         s.landed(copy)
 
@@ -286,10 +334,6 @@
         q = q + qr_v[2, rows, :].astype(F32) + qr_v[3, rows, :].astype(F32)
         q_v[rows, :] = q.astype(BF)
 
-    for copy, j in cap_in:
-        s.landed(copy)
-        block = cap_v.at[c, j]
-        cap_pair.append(s.send(block, block, pair))
     for copy in wkv_in:
         s.done(copy)
 
@@ -302,7 +346,7 @@
         s.landed(copy)
     key_value(1 - c)
     for i in (0, 1):
-        p = flags[i : i + 1, :]
+        p = one[i]
         both = kv_v[0].astype(F32) * p + kv_v[1].astype(F32) * (1.0 - p)
         sel_v[i] = both.astype(BF)
     kv_in = [s.send(sel_v.at[q // 2], kvr_v.at[mine], to) for to, q in quad_peers(*place)]
@@ -318,7 +362,8 @@
         q, g = q_v[:, cols], gs_v[:, cols]
         k, v = kvr_v[h, :, :HD], kvr_v[h, :, HD:]
         scores = lax.dot_general(q, k, NT, preferred_element_type=F32) * inv_root
-        scores = jnp.where(flags[2:3, :] > 0.5, scores, -1e30)
+        live = lax.broadcasted_iota(jnp.int32, scores.shape, 1) < length
+        scores = jnp.where(live, scores, -1e30)
         e = jnp.exp(scores - jnp.max(scores, axis=-1, keepdims=True))
         probs = e / jnp.sum(e, axis=-1, keepdims=True)
         probs_b = probs.astype(BF)
@@ -331,12 +376,45 @@
         gkv_v[h, :, :HD] = gk.astype(BF)
         gkv_v[h, :, HD:] = gv.astype(BF)
 
-    gq_in = [s.send(gq_v, gqa_v.at[:, span(x, 512)], to) for to, _ in xp]
-    gq_in.append(s.send(gq_v, gqa_v.at[:, span(x, 512)], None))
+    right, left = xp[0][0], xp[2][0]
+
+    def part(who, half):
+        return gqa_v.at[pl.ds(half * 256, 256), span(who, 512)]
+
+    def own_part(half):
+        return gq_v.at[pl.ds(half * 256, 256)]
+
+    to_right = [s.send(own_part(h), part(x, h), right) for h in (0, 1)]
+    to_left = [s.send(own_part(h), part(x, h), left) for h in (1, 0)]
+    gq_in = [s.send(gq_v, gqa_v.at[:, span(x, 512)], None), to_right[1], to_left[1]]
     gkv_in = [
         s.send(gkv_v.at[q], gkvr_v.at[mine], to) for to, q in quad_peers(*place)
     ]
     gkvr_v[mine] = gkv_v[mine]
+    for copy in gkv_in:
+        s.landed(copy)
+    im0 = gkvr_v[0].astype(F32) + gkvr_v[1].astype(F32)
+    im1 = gkvr_v[2].astype(F32) + gkvr_v[3].astype(F32)
+    p0, p1 = one
+    gkvs_v[:LCAP, :] = (im0 * p0 + im1 * p1).astype(BF)
+    gkvs_v[LCAP:, :] = (im0 * (1.0 - p0) + im1 * (1.0 - p1)).astype(BF)
+
+    def kv_block(j):
+        cols = span(j, 512)
+        rows = cap_v[:, :, :, cols].reshape(512, 512)
+        kvp_v[j] = lax.dot_general(rows, gkvs_v[...], TN, preferred_element_type=F32).astype(BF)
+
+    kv_sum_in = []
+    here_dp = y * 2 + zh
+    for k, (to, j) in enumerate(dp_peers(*place)):
+        kv_block(j)
+        kv_sum_in.append(s.send(kvp_v.at[j], kvs_v.at[k], to))
+    kv_block(here_dp)
+
+    s.landed(to_right[0])
+    gq_in.append(s.send(part((x + 3) % 4, 0), part((x + 3) % 4, 0), right))
+    s.landed(to_left[0])
+    gq_in.append(s.send(part((x + 1) % 4, 1), part((x + 1) % 4, 1), left))
     for to, v in xp + [(None, x)]:
         for half in (0, 1):
             s.send(
@@ -344,25 +422,6 @@
                 attn_out.at[:, span(half * 4 + x, 256)],
                 to,
             )
-    for copy in gkv_in:
-        s.landed(copy)
-    im0 = gkvr_v[0].astype(F32) + gkvr_v[1].astype(F32)
-    im1 = gkvr_v[2].astype(F32) + gkvr_v[3].astype(F32)
-    p0, p1 = flags[0:1, :], flags[1:2, :]
-    gkvs_v[:LCAP, :] = (im0 * p0 + im1 * p1).astype(BF)
-    gkvs_v[LCAP:, :] = (im0 * (1.0 - p0) + im1 * (1.0 - p1)).astype(BF)
-
-    def kv_block(j):
-        cols = span(j, 512)
-        rows = cap_v[:, :, :, cols].reshape(512, 512)
-        kvp_v[j] = lax.dot_general(rows, gkvs_v[...], TN, preferred_element_type=F32).astype(BF)
-
-    kv_sum_in = []
-    here_dp = y * 2 + zh
-    for k, (to, j) in enumerate(dp_peers(*place)):
-        kv_block(j)
-        kv_sum_in.append(s.send(kvp_v.at[j], kvs_v.at[k], to))
-    kv_block(here_dp)
 
     for copy in gq_in:
         s.landed(copy)
@@ -431,7 +490,8 @@
             total = total + kvs_v[k, rows, :].astype(F32)
         kvp_v[here_dp, rows, :] = total.astype(BF)
 
-    for to, _ in dp_peers(*place) + [(None, 0)]:
+    spread = [to for to, _ in dp_peers(*place)] + [None]
+    for to in spread[:3]:
         s.send(kvp_v.at[here_dp], gkv_out.at[here_dp], to)
 
     for copy in r1_in + r2_in:
@@ -452,6 +512,8 @@
         s.send(s1_v.at[(t % 2) * 2 + t // 2], t1_v.at[k], to) for k, (to, t) in enumerate(zp)
     ]
     t_in += [s.send(s2_v.at[v], t2_v.at[k], to) for k, (to, v) in enumerate(yp)]
+    for to in spread[3:]:
+        s.send(kvp_v.at[here_dp], gkv_out.at[here_dp], to)
     for copy in t_in:
         s.landed(copy)
     left, right = s1_v[at].astype(F32), s2_v[y].astype(F32)
@@ -466,7 +528,7 @@
 
 
 GROUPS = (chip_peers, quad_peers, dp_peers, z_peers)
-COPIES = 150
+COPIES = 180
 
 
 def main(*ins):
@@ -475,7 +537,7 @@
     scratch = [
         (128, 4096), (128, 4096), (256, 2048), (4, 128, 4096), (32, 4096), (4096, 768), (384, 4096),
         (4096, 256), (1024, 2048), (512, 1024), (512, 512), None, (512, 384),
-        (256, 4096), (256, 4096), (256, 4096), (8, 32, 4096), (3, 512, 512), (4, 512, 512),
+        (256, 4096), (256, 4096), (256, 4096), (4, 32, 4096), (3, 32, 4096), (3, 512, 512), (4, 512, 512),
         (512, 512), (2, 8, 32, 4096), (2, LCAP, 256), (2, LCAP, 256), (4, LCAP, 256),
         (512, 512), (512, 512), (4, LCAP, 256), (4, LCAP, 256), (512, 256), (8, 512, 256),
         (512, 2048), (4, 128, 2048), (3, 4, 32, 1024), (3, 128, 1024), (4, 32, 1024), (4, 32, 1024),
@@ -484,7 +546,7 @@
     return pl.pallas_call(
         kernel,
         out_shape=[jax.ShapeDtypeStruct(shape, BF) for shape in shapes],
-        in_specs=[anys] * 9 + [vmem] * 3,
+        in_specs=[anys] * 9 + [vmem] * 2 + [pl.BlockSpec(memory_space=pltpu.SMEM)] * 2,
         out_specs=[anys] * 4,
         scratch_shapes=[
             pltpu.VMEM((512, 768), F32) if shape is None else pltpu.VMEM(shape, BF)
@@ -498,54 +560,104 @@
     )(*ins)
 
 
-def last_kernel(attn, dxn, lat, gq, gkv, attn_o, lat_o, gq_o, gk_o, gv_o):
-    attn_o[...] = attn[...].astype(F32)
-    v = lat[...].astype(F32)
-    r = v - jnp.mean(v, axis=-1, keepdims=True)
-    rstd = lax.rsqrt(jnp.mean(r * r, axis=-1, keepdims=True) + 1e-06)
-    xhat = r * rstd
-    g = dxn[...].astype(F32)
-    lat_o[...] = rstd * (
-        g
-        - jnp.mean(g, axis=-1, keepdims=True)
-        - xhat * jnp.mean(g * xhat, axis=-1, keepdims=True)
-    )
-    for w in range(4):
-        for h in (0, 1):
-            there, here = h * 1024 + w * 256, w * 512 + h * 256
-            gq_o[:, there : there + 256] = gq[0, :, here : here + 256].astype(F32)
-    gk_o[...] = gkv[0, :, :HD].astype(F32)
-    gv_o[...] = gkv[0, :, HD:].astype(F32)
-
-
-def last(attn, dxn, lat, gq, gkv):
-    def rows(count, width):
-        return pl.BlockSpec((count, width), lambda i: (i, 0))
-
+def last_kernel(
+    attn, dxn, lat, gq, gkv, attn_o, lat_o, gq_o, gk_o, gv_o,
+    attn_v, dxn_v, lat_v, gq_v, gkv_v, attn_f, lat_f, gq_f, gk_f, gv_f, sems,
+):
+    copies = []
+
+    def move(src, dst):
+        copy = pltpu.make_async_copy(src, dst, sems.at[len(copies)])
+        copy.start()
+        copies.append(copy)
+        return copy
+
+    def part(i, size):
+        return pl.ds(i * size, size)
+
+    outs = []
+    kv_in = [move(gkv.at[part(i, 2)], gkv_v.at[part(i, 2)]) for i in range(4)]
+    lat_in = []
+    for i in range(4):
+        rows = part(i, 32)
+        lat_in.append(
+            (move(lat.at[rows], lat_v.at[rows]), move(dxn.at[rows], dxn_v.at[rows]))
+        )
+    gq_in = [move(gq.at[part(i, 4)], gq_v.at[part(i, 4)]) for i in (0, 1)]
+    attn_in = move(attn, attn_v)
+    for i in range(4):
+        kv_in[i].wait()
+
+        @pl.loop(0, 8)
+        def _(n, i=i):
+            at, rows = i * 2 + n // 4, pl.ds(pl.multiple_of((n % 4) * 128, 128), 128)
+            to = pl.ds(pl.multiple_of(i * 1024 + n * 128, 128), 128)
+            gk_f[to, :] = gkv_v[at, rows, :HD].astype(F32)
+            gv_f[to, :] = gkv_v[at, rows, HD:].astype(F32)
+
+        rows = part(i, 1024)
+        outs += [move(gk_f.at[rows], gk_o.at[rows]), move(gv_f.at[rows], gv_o.at[rows])]
+    for i in range(4):
+        for copy in lat_in[i]:
+            copy.wait()
+
+        @pl.loop(0, 2)
+        def _(n, i=i):
+            rows = pl.ds(pl.multiple_of(i * 32 + n * 16, 16), 16)
+            v = lat_v[rows, :].astype(F32)
+            r = v - jnp.mean(v, axis=-1, keepdims=True)
+            rstd = lax.rsqrt(jnp.mean(r * r, axis=-1, keepdims=True) + 1e-06)
+            xhat = r * rstd
+            g = dxn_v[rows, :].astype(F32)
+            lat_f[rows, :] = rstd * (
+                g
+                - jnp.mean(g, axis=-1, keepdims=True)
+                - xhat * jnp.mean(g * xhat, axis=-1, keepdims=True)
+            )
+
+        rows = part(i, 32)
+        outs.append(move(lat_f.at[rows], lat_o.at[rows]))
+    for i in (0, 1):
+        gq_in[i].wait()
+
+        @pl.loop(0, 4)
+        def _(n, i=i):
+            rows = pl.ds(pl.multiple_of((i * 4 + n) * 32, 32), 32)
+            for w in range(4):
+                for h in (0, 1):
+                    there, here = h * 1024 + w * 256, w * 512 + h * 256
+                    gq_f[rows, there : there + 256] = gq_v[i * 4 + n, :, here : here + 256].astype(
+                        F32
+                    )
+
+        rows = part(i, 128)
+        outs.append(move(gq_f.at[rows], gq_o.at[rows]))
+    attn_in.wait()
+
+    @pl.loop(0, 4)
+    def _(n):
+        rows = pl.ds(pl.multiple_of(n * 32, 32), 32)
+        attn_f[rows, :] = attn_v[rows, :].astype(F32)
+
+    outs.append(move(attn_f, attn_o))
+    for copy in outs:
+        copy.wait()
+
+
+def last(*ins):
+    anys = pl.BlockSpec(memory_space=pl.ANY)
+    shapes = [(128, 2048), (128, 4096), (256, 2048), (4096, HD), (4096, HD)]
     return pl.pallas_call(
         last_kernel,
-        grid=(8,),
-        out_shape=[
-            jax.ShapeDtypeStruct(shape, F32)
-            for shape in [(128, 2048), (128, 4096), (256, 2048), (4096, HD), (4096, HD)]
-        ],
-        in_specs=[
-            rows(16, 2048),
-            rows(16, 4096),
-            rows(16, 4096),
-            pl.BlockSpec((1, 32, 2048), lambda i: (i, 0, 0)),
-            pl.BlockSpec((1, 512, 256), lambda i: (i, 0, 0)),
-        ],
-        out_specs=[
-            rows(16, 2048),
-            rows(16, 4096),
-            rows(32, 2048),
-            rows(512, HD),
-            rows(512, HD),
-        ],
-        compiler_params=pltpu.CompilerParams(vmem_limit_bytes=32 * 2**20),
+        out_shape=[jax.ShapeDtypeStruct(shape, F32) for shape in shapes],
+        in_specs=[anys] * 5,
+        out_specs=[anys] * 5,
+        scratch_shapes=[pltpu.VMEM(a.shape, BF) for a in ins]
+        + [pltpu.VMEM(shape, F32) for shape in shapes]
+        + [pltpu.SemaphoreType.DMA((40,))],
+        compiler_params=pltpu.CompilerParams(vmem_limit_bytes=63 * 2**20),
         name="last",
-    )(attn, dxn, lat, gq, gkv)
+    )(*ins)
 
 
 def local(
@@ -563,12 +675,6 @@
     caption_of_image,
     grad_out,
 ):
-    zl = lax.axis_index("fsdp") // 8
-    first = (caption_of_image == 0).astype(F32)
-    mine = lax.dynamic_index_in_dim(caption_of_image, zl, 0)
-    length = jnp.where(mine == 0, cap_lengths[:1], cap_lengths[1:])
-    live = (jnp.arange(LCAP, dtype=jnp.int32) < length).astype(F32)
-    flags = jnp.concatenate([jnp.broadcast_to(first[:, None], (2, LCAP)), live[None]])
     attn, dxn, gq, gkv = main(
         latents,
         grad_out,
@@ -579,9 +685,10 @@
         t5_wo,
         w_key,
         w_value,
-        t5_norm_gain[None],
-        t5_final_gain[None],
-        flags,
+        t5_norm_gain,
+        t5_final_gain,
+        cap_lengths,
+        caption_of_image,
     )
     return last(attn, dxn, latents, gq, gkv)
 

time: 249 us -> 210 us (0.84)
  the two profiles are of different devices: /device:TPU:2 before, /device:TPU:0 now
where the time goes in v4:
time: 210 us; the launch traced here: 208 us
  Pallas kernels  207 us (99%)
    pallas_call x1, Pallas kernels, main(): pl.pallas_call(kernel, out_shape=[jax.ShapeDtypeStruct(shape, BF) for sha...  200 us
    pallas_call x1, Pallas kernels, last(): pl.pallas_call(last_kernel, out_shape=[jax.ShapeDtypeStruct(shape, F32) f...  6.82 us

profile of v4, /device:TPU:0, one launch (start us, length us, event | category | flops | bytes accessed | tf_op | source)
XLA Modules:
  0.0 207.9 jit_solution(5918530060778155829)
XLA Ops:
  0.6 200.5 %main.1 = (bf16[128,2048]{1,0:T(8,128)(2,1)}, bf16[128,4096]{1,0:T(8,128)(2,1)}, bf16[8,32,2048]{2,1,0:T(8,128)(2,1)}, bf16[8,512,256]{2,1,0:T(8,128)(2,1)}) custom-call(bf16[128,4096]{1,0:T(8,128)(2,1)} %lat.3, bf16[128,2048]{1,0:T(8,128)(2,1)} %go.1, bf16[256,2048]{1,0:T(8,128)(2,1)} %wq.1, bf16[512,4096]{1,0:T(8,128)(2,1)} %ch.1, bf16[4096,384]{1,0:T(8,128)(2,1)} %wi0.1, ...), custom_call_target="tpu_custom_call" | custom-call | tf_op jit(solution)/shard_map/main/pallas_call | solution.py:546
  201.1 6.8 %last.1 = (f32[128,2048]{1,0:T(8,128)}, f32[128,4096]{1,0:T(8,128)}, f32[256,2048]{1,0:T(8,128)}, f32[4096,128]{1,0:T(8,128)}, f32[4096,128]{1,0:T(8,128)}) custom-call(bf16[128,2048]{1,0:T(8,128)(2,1)} %get-tuple-element.9.attn, bf16[128,4096]{1,0:T(8,128)(2,1)} %get-tuple-element.10.dxn, bf16[128,4096]{1,0:T(8,128)(2,1)} %lat.3, ...), custom_call_target="tpu_custom_call" | custom-call | tf_op jit(solution)/shard_map/last/pallas_call | solution.py:650

commit v5 on v4

--- a/solution.py
+++ b/solution.py
@@ -36,16 +36,6 @@
     z = zh * 2 + zl
     there = [(z + k) % 4 for k in (1, 2, 3)]
     return [(device(y, t // 2, t % 2, x, c), t) for t in there]
-
-
-def dp_peers(y, zh, zl, x, c):
-    there = [((y + k) % 4, (zh + a) % 2) for a in (0, 1) for k in range(4) if a or k]
-    return [(device(v, w, zl, x, c), v * 2 + w) for v, w in there]
-
-
-def chip_peers(y, zh, zl, x, c):
-    there = [((zl + a) % 2, (x + k) % 4) for a in (0, 1) for k in range(4) if a or k]
-    return [(device(y, zh, w, v, c), w * 4 + v) for w, v in there]
 
 
 def quad_peers(y, zh, zl, x, c):
@@ -112,7 +102,7 @@
     lat_v, xn_v, wp_v, ch_v, row_v, wi_v, wo_v, wkv_v, wx_v, xs_v, gs_v, gl_v, hid_v,
     give_v, keep_v, rc_v, fz_v, fr_v, qs_v, qr_v, q_v, cap_v, kv_v, sel_v, kvr_v,
     attn_v, gq_v, gkv_v, gkvr_v, gkvs_v, kvp_v, gqa_v, grc_v, r1_v, r2_v, s1_v, s2_v, t1_v, t2_v,
-    fin_v, kvs_v, sems_a, sems_b,
+    fin_v, ka_v, kb_v, k2a_v, k2b_v, sems_a, sems_b,
 ):
     place = coords()
     y, zh, zl, x, c = place
@@ -393,6 +383,10 @@
     gkvr_v[mine] = gkv_v[mine]
     for copy in gkv_in:
         s.landed(copy)
+    s.landed(to_right[0])
+    gq_in.append(s.send(part((x + 3) % 4, 0), part((x + 3) % 4, 0), right))
+    s.landed(to_left[0])
+    gq_in.append(s.send(part((x + 1) % 4, 1), part((x + 1) % 4, 1), left))
     im0 = gkvr_v[0].astype(F32) + gkvr_v[1].astype(F32)
     im1 = gkvr_v[2].astype(F32) + gkvr_v[3].astype(F32)
     p0, p1 = one
@@ -404,17 +398,19 @@
         rows = cap_v[:, :, :, cols].reshape(512, 512)
         kvp_v[j] = lax.dot_general(rows, gkvs_v[...], TN, preferred_element_type=F32).astype(BF)
 
-    kv_sum_in = []
+    yp, zp = y_peers(*place), z_peers(*place)
+    zpair = device(y, 1 - zh, zl, x, c)
     here_dp = y * 2 + zh
-    for k, (to, j) in enumerate(dp_peers(*place)):
-        kv_block(j)
-        kv_sum_in.append(s.send(kvp_v.at[j], kvs_v.at[k], to))
-    kv_block(here_dp)
-
-    s.landed(to_right[0])
-    gq_in.append(s.send(part((x + 3) % 4, 0), part((x + 3) % 4, 0), right))
-    s.landed(to_left[0])
-    gq_in.append(s.send(part((x + 1) % 4, 1), part((x + 1) % 4, 1), left))
+    first, second = pl.ds(0, 256), pl.ds(256, 256)
+    ka_in, kb_in = [], []
+    for k in (1, 3, 2, 0):
+        v = (y + k) % 4
+        kv_block(v * 2 + 1 - zh)
+        ka_in.append(s.send(kvp_v.at[v * 2 + 1 - zh, first], ka_v.at[v], zpair))
+        kv_block(v * 2 + zh)
+        if k:
+            both = kvp_v.at[pl.ds(v * 2, 2), second]
+            kb_in.append(s.send(both, kb_v.at[k - 1], yp[k - 1][0]))
     for to, v in xp + [(None, x)]:
         for half in (0, 1):
             s.send(
@@ -422,6 +418,22 @@
                 attn_out.at[:, span(half * 4 + x, 256)],
                 to,
             )
+
+    for copy in ka_in + kb_in:
+        s.landed(copy)
+    k2a_in = []
+    for k in (1, 3, 2, 0):
+        v = (y + k) % 4
+        total = kvp_v[v * 2 + zh, first, :].astype(F32) + ka_v[v].astype(F32)
+        kvp_v[v * 2 + zh, first, :] = total.astype(BF)
+        if k:
+            k2a_in.append(s.send(kvp_v.at[v * 2 + zh, first], k2a_v.at[k - 1], yp[k - 1][0]))
+    for w in (1 - zh, zh):
+        total = kvp_v[y * 2 + w, second, :].astype(F32)
+        for k in range(3):
+            total = total + kb_v[k, w].astype(F32)
+        kvp_v[y * 2 + w, second, :] = total.astype(BF)
+    k2b_in = s.send(kvp_v.at[y * 2 + 1 - zh, second], k2b_v, zpair)
 
     for copy in gq_in:
         s.landed(copy)
@@ -469,7 +481,6 @@
         keep = ch_v[i // 8, rows, 2048:].astype(F32) + grc_v[i // 8, rows, :].astype(F32)
         ch_v[i // 8, rows, 2048:] = keep.astype(BF)
 
-    yp, zp = y_peers(*place), z_peers(*place)
     r1_in = [
         s.send(ch_v.at[:, span(v, 32), pl.ds(2048, 1024)], r1_v.at[k], to)
         for k, (to, v) in enumerate(yp)
@@ -479,21 +490,39 @@
         for k, (to, t) in enumerate(zp)
     ]
 
-    for copy in kv_sum_in:
-        s.landed(copy)
-
-    @pl.loop(0, 8)
-    def _(i):
-        rows = pl.ds(pl.multiple_of(i * 64, 64), 64)
-        total = kvp_v[here_dp, rows, :].astype(F32)
-        for k in range(7):
-            total = total + kvs_v[k, rows, :].astype(F32)
-        kvp_v[here_dp, rows, :] = total.astype(BF)
-
-    spread = [to for to, _ in dp_peers(*place)] + [None]
-    for to in spread[:3]:
-        s.send(kvp_v.at[here_dp], gkv_out.at[here_dp], to)
-
+    for copy in k2a_in + [k2b_in]:
+        s.landed(copy)
+    total = kvp_v[here_dp, first, :].astype(F32)
+    for k in range(3):
+        total = total + k2a_v[k].astype(F32)
+    kvp_v[here_dp, first, :] = total.astype(BF)
+    total = kvp_v[here_dp, second, :].astype(F32) + k2b_v[...].astype(F32)
+    kvp_v[here_dp, second, :] = total.astype(BF)
+
+    def kv_at(v, w):
+        return gkv_out.at[v * 2 + w]
+
+    def q_at(v, w):
+        return gq_out.at[w * 4 + v]
+
+    def spread(own, out, rows):
+        s.send(own, out(y, zh), None)
+        over = s.send(own.at[pl.ds(0, rows)], out(y, zh).at[pl.ds(0, rows)], zpair)
+        along = [(k, s.send(own, out(y, zh), yp[k - 1][0])) for k in (1, 3, 2)]
+        s.send(own.at[pl.ds(rows, rows)], out(y, zh).at[pl.ds(rows, rows)], zpair)
+        return over, along
+
+    def pass_first(over, out, rows):
+        s.landed(over)
+        for k in (1, 3, 2):
+            pass_on(out(y, 1 - zh).at[pl.ds(0, rows)], yp[k - 1][0])
+
+    def pass_second(along, out, rows):
+        for k, copy in along:
+            s.landed(copy)
+            pass_on(out((y + 4 - k) % 4, zh).at[pl.ds(rows, rows)], zpair)
+
+    kv_over, kv_along = spread(kvp_v.at[here_dp], kv_at, 256)
     for copy in r1_in + r2_in:
         s.landed(copy)
     for i in range(4):
@@ -512,8 +541,7 @@
         s.send(s1_v.at[(t % 2) * 2 + t // 2], t1_v.at[k], to) for k, (to, t) in enumerate(zp)
     ]
     t_in += [s.send(s2_v.at[v], t2_v.at[k], to) for k, (to, v) in enumerate(yp)]
-    for to in spread[3:]:
-        s.send(kvp_v.at[here_dp], gkv_out.at[here_dp], to)
+    pass_first(kv_over, kv_at, 256)
     for copy in t_in:
         s.landed(copy)
     left, right = s1_v[at].astype(F32), s2_v[y].astype(F32)
@@ -522,12 +550,14 @@
         right = right + t2_v[k].astype(F32)
     fin_v[:, :1024] = left.astype(BF)
     fin_v[:, 1024:] = right.astype(BF)
-    for to, _ in dp_peers(*place) + [(None, 0)]:
-        s.send(fin_v, gq_out.at[zh * 4 + y], to)
+    q_over, q_along = spread(fin_v, q_at, 16)
+    pass_second(kv_along, kv_at, 256)
+    pass_first(q_over, q_at, 16)
+    pass_second(q_along, q_at, 16)
     s.finish()
 
 
-GROUPS = (chip_peers, quad_peers, dp_peers, z_peers)
+GROUPS = (x_peers, quad_peers, y_peers, z_peers)
 COPIES = 180
 
 
@@ -541,7 +571,8 @@
         (512, 512), (2, 8, 32, 4096), (2, LCAP, 256), (2, LCAP, 256), (4, LCAP, 256),
         (512, 512), (512, 512), (4, LCAP, 256), (4, LCAP, 256), (512, 256), (8, 512, 256),
         (512, 2048), (4, 128, 2048), (3, 4, 32, 1024), (3, 128, 1024), (4, 32, 1024), (4, 32, 1024),
-        (3, 32, 1024), (3, 32, 1024), (32, 2048), (7, 512, 256),
+        (3, 32, 1024), (3, 32, 1024), (32, 2048), (4, 256, 256), (3, 2, 256, 256),
+        (3, 256, 256), (256, 256),
     ]
     return pl.pallas_call(
         kernel,

time: 210 us -> 187 us (0.89); the launches traced: 208 us -> 187 us
  Pallas kernels: 207 us -> 187 us
    pallas_call x1, Pallas kernels: 200 us -> 180 us  [main(): pl.pallas_call(kernel, out_shape=[jax.ShapeDtypeStruct(shape, BF) for sha...]
where the time goes in v5:
time: 187 us
  Pallas kernels  187 us (100%)
    pallas_call x1, Pallas kernels, main(): pl.pallas_call(kernel, out_shape=[jax.ShapeDtypeStruct(shape, BF) for sha...  180 us
    pallas_call x1, Pallas kernels, last(): pl.pallas_call(last_kernel, out_shape=[jax.ShapeDtypeStruct(shape, F32) f...  6.82 us

profile of v5, /device:TPU:0, one launch (start us, length us, event | category | flops | bytes accessed | tf_op | source)
XLA Modules:
  0.0 187.2 jit_solution(5960588933201723378)
XLA Ops:
  0.6 179.8 %main.1 = (bf16[128,2048]{1,0:T(8,128)(2,1)}, bf16[128,4096]{1,0:T(8,128)(2,1)}, bf16[8,32,2048]{2,1,0:T(8,128)(2,1)}, bf16[8,512,256]{2,1,0:T(8,128)(2,1)}) custom-call(bf16[128,4096]{1,0:T(8,128)(2,1)} %lat.3, bf16[128,2048]{1,0:T(8,128)(2,1)} %go.1, bf16[256,2048]{1,0:T(8,128)(2,1)} %wq.1, bf16[512,4096]{1,0:T(8,128)(2,1)} %ch.1, bf16[4096,384]{1,0:T(8,128)(2,1)} %wi0.1, ...), custom_call_target="tpu_custom_call" | custom-call | tf_op jit(solution)/shard_map/main/pallas_call | solution.py:577
  180.4 6.8 %last.1 = (f32[128,2048]{1,0:T(8,128)}, f32[128,4096]{1,0:T(8,128)}, f32[256,2048]{1,0:T(8,128)}, f32[4096,128]{1,0:T(8,128)}, f32[4096,128]{1,0:T(8,128)}) custom-call(bf16[128,2048]{1,0:T(8,128)(2,1)} %get-tuple-element.9.attn, bf16[128,4096]{1,0:T(8,128)(2,1)} %get-tuple-element.10.dxn, bf16[128,4096]{1,0:T(8,128)(2,1)} %lat.3, ...), custom_call_target="tpu_custom_call" | custom-call | tf_op jit(solution)/shard_map/last/pallas_call | solution.py:681

commit v6 on v5

--- a/solution.py
+++ b/solution.py
@@ -100,7 +100,7 @@
     lat, go, wq, ch, wi0, wi1, wo, wk, wv, gain, gain2, lengths, owner,
     attn_out, dxn_out, gq_out, gkv_out,
     lat_v, xn_v, wp_v, ch_v, row_v, wi_v, wo_v, wkv_v, wx_v, xs_v, gs_v, gl_v, hid_v,
-    give_v, keep_v, rc_v, fz_v, fr_v, qs_v, qr_v, q_v, cap_v, kv_v, sel_v, kvr_v,
+    give_v, keep_v, rc_v, fz_v, fr_v, qs_v, qh_v, qr_v, q_v, cap_v, kv_v, sel_v, kvr_v,
     attn_v, gq_v, gkv_v, gkvr_v, gkvs_v, kvp_v, gqa_v, grc_v, r1_v, r2_v, s1_v, s2_v, t1_v, t2_v,
     fin_v, ka_v, kb_v, k2a_v, k2b_v, sems_a, sems_b,
 ):
@@ -116,12 +116,16 @@
     mine_first = 1 - jnp.minimum(owner[zl], 1)
     length = lengths[0] * mine_first + lengths[1] * (1 - mine_first)
 
+    barrier = pltpu.get_barrier_semaphore()
+    peers = [to for group in GROUPS for to, _ in group(*place)]
+    for to in peers:
+        pl.semaphore_signal(barrier, inc=1, device_id=to, device_id_type=MESH)
+    lat_in = s.send(lat, lat_v, None)
     perm = [
         s.send(wq.at[:, pl.ds(h * 1024 + v * 256, 256)], wp_v.at[:, pl.ds(v * 512 + h * 256, 256)], None)
         for h in (0, 1)
         for v in range(4)
     ]
-    lat_in = s.send(lat, lat_v, None)
     ch_in = [s.send(ch.at[pl.ds(i * 128, 128)], ch_v.at[i], None) for i in range(4)]
     wi_in = [
         s.send(wi0, wi_v.at[:, pl.ds(0, 384)], None),
@@ -132,21 +136,6 @@
         s.send(wk, wkv_v.at[:, pl.ds(0, 128)], None),
         s.send(wv, wkv_v.at[:, pl.ds(128, 128)], None),
     ]
-    barrier = pltpu.get_barrier_semaphore()
-    peers = [to for group in GROUPS for to, _ in group(*place)]
-    for to in peers:
-        pl.semaphore_signal(barrier, inc=1, device_id=to, device_id_type=MESH)
-    pl.semaphore_wait(barrier, len(peers))
-
-    for copy in perm:
-        s.done(copy)
-    w_over = [
-        s.send(wp_v.at[pl.ds(i * 128, 128)], wx_v.at[span(mine * 2 + i, 128)], to)
-        for i, to in enumerate((across, behind))
-    ]
-    w_pair = s.send(wp_v, wx_v.at[span(mine, 256)], pair)
-    w_own = s.send(wp_v, wx_v.at[span(mine, 256)], None)
-
     s.done(lat_in)
 
     @pl.loop(0, 8)
@@ -156,6 +145,7 @@
         r = v - jnp.mean(v, axis=-1, keepdims=True)
         xn_v[rows, :] = (r * lax.rsqrt(jnp.mean(r * r, axis=-1, keepdims=True) + 1e-06)).astype(BF)
 
+    pl.semaphore_wait(barrier, len(peers))
     x_in, g_in = [], []
     for to, v in xp + [(None, x)]:
         for half in (0, 1):
@@ -166,15 +156,14 @@
                     to,
                 )
             )
-    for to, v in xp + [(None, x)]:
-        for half in (0, 1):
-            g_in.append(
-                s.send(
-                    go.at[:, span(half * 4 + v, 256)],
-                    gs_v.at[span(x, 128), pl.ds(half * 256, 256)],
-                    to,
-                )
-            )
+    for copy in perm:
+        s.done(copy)
+    w_over = [
+        s.send(wp_v.at[pl.ds(i * 128, 128)], wx_v.at[span(mine * 2 + i, 128)], to)
+        for i, to in enumerate((across, behind))
+    ]
+    w_pair = s.send(wp_v, wx_v.at[span(mine, 256)], pair)
+    w_own = s.send(wp_v, wx_v.at[span(mine, 256)], None)
 
     for copy in ch_in:
         s.done(copy)
@@ -198,44 +187,6 @@
         cols = pl.ds(pl.multiple_of((i % 3) * 256, 256), 256)
         normed = ch_v[pl.ds((i // 3) * 2, 2)].reshape(256, 4096)
         gl_v[rows, cols] = jnp.dot(normed, wi_v[:, cols], preferred_element_type=F32)
-
-    @pl.loop(0, 8)
-    def _(i):
-        rows = pl.ds(pl.multiple_of(i * 64, 64), 64)
-        g, u = gl_v[rows, :384], gl_v[rows, 384:]
-        hid_v[rows, :] = (jax.nn.gelu(g, approximate=True) * u).astype(BF)
-
-    s.done(wo_in)
-
-    def term(which, out):
-        rows = span(which, 256)
-
-        @pl.loop(0, 8)
-        def _(i):
-            cols = pl.ds(pl.multiple_of(i * 512, 512), 512)
-            out[:, cols] = jnp.dot(
-                hid_v[rows, :], wo_v[:, cols], preferred_element_type=F32
-            ).astype(BF)
-
-    term(1 - c, give_v)
-    ff_pair = s.send(give_v, rc_v, pair)
-    term(c, keep_v)
-    s.landed(ff_pair)
-
-    def add_core(z):
-        @pl.loop(0, 8)
-        def _(i):
-            rows = pl.ds(pl.multiple_of(z * 128 + i * 16, 16), 16)
-            total = keep_v[rows, :].astype(F32) + rc_v[rows, :].astype(F32)
-            keep_v[rows, :] = total.astype(BF)
-
-    add_core(1 - zl)
-    order = [1, 3, 2, 0]
-    fz_in = [
-        s.send(keep_v.at[span((1 - zl) * 4 + (x + k) % 4, 32)], fz_v.at[(x + k) % 4], across)
-        for k in order
-    ]
-    add_core(zl)
 
     for copy in w_over:
         s.landed(copy)
@@ -254,11 +205,68 @@
                 xs_v[rows, :], wx_v[:, from_cols], preferred_element_type=F32
             ).astype(BF)
 
-    q_in = []
-    for k in (0, 2):
-        query_block(xp[k][1], qs_v, k)
-        q_in.append(s.send(qs_v.at[k], qr_v.at[x], xp[k][0]))
-
+    right, left = xp[0][0], xp[2][0]
+    upper, lower = pl.ds(0, 256), pl.ds(256, 256)
+    query_block(xp[1][1], qs_v, 1)
+    qh_in = [
+        s.send(qs_v.at[1, upper], qh_v.at[0], right),
+        s.send(qs_v.at[1, lower], qh_v.at[1], left),
+    ]
+    query_block(xp[0][1], qs_v, 0)
+    q_in = [s.send(qs_v.at[0, lower], qr_v.at[1, lower], right)]
+    query_block(xp[2][1], qs_v, 2)
+    q_in.append(s.send(qs_v.at[2, upper], qr_v.at[2, upper], left))
+
+    def pass_query(n, slot, rows, to):
+        s.landed(qh_in[n])
+        total = qs_v[slot, rows, :].astype(F32) + qh_v[n].astype(F32)
+        qs_v[slot, rows, :] = total.astype(BF)
+        q_in.append(s.send(qs_v.at[slot, rows], qr_v.at[1 + n, rows], to))
+
+    @pl.loop(0, 8)
+    def _(i):
+        rows = pl.ds(pl.multiple_of(i * 64, 64), 64)
+        g, u = gl_v[rows, :384], gl_v[rows, 384:]
+        hid_v[rows, :] = (jax.nn.gelu(g, approximate=True) * u).astype(BF)
+
+    s.done(wo_in)
+
+    def term(which, z, out):
+        rows, to_rows = span(which * 2 + z, 128), span(z, 128)
+
+        @pl.loop(0, 4)
+        def _(i):
+            cols = pl.ds(pl.multiple_of(i * 1024, 1024), 1024)
+            out[to_rows, cols] = jnp.dot(
+                hid_v[rows, :], wo_v[:, cols], preferred_element_type=F32
+            ).astype(BF)
+
+    pair_in = []
+    for z in (1 - zl, zl):
+        term(1 - c, z, give_v)
+        pair_in.append(s.send(give_v.at[span(z, 128)], rc_v.at[span(z, 128)], pair))
+
+    def add_core(z):
+        @pl.loop(0, 8)
+        def _(i):
+            rows = pl.ds(pl.multiple_of(z * 128 + i * 16, 16), 16)
+            total = keep_v[rows, :].astype(F32) + rc_v[rows, :].astype(F32)
+            keep_v[rows, :] = total.astype(BF)
+
+    term(c, 1 - zl, keep_v)
+    s.landed(pair_in[0])
+    add_core(1 - zl)
+    order = [1, 3, 2, 0]
+    fz_in = [
+        s.send(keep_v.at[span((1 - zl) * 4 + (x + k) % 4, 32)], fz_v.at[(x + k) % 4], across)
+        for k in order
+    ]
+    term(c, zl, keep_v)
+    s.landed(pair_in[1])
+    add_core(zl)
+
+    pass_query(0, 0, upper, right)
+    pass_query(1, 2, lower, left)
     ff_in = []
 
     def add_across(n):
@@ -273,12 +281,10 @@
         return total
 
     add_across(0)
-    query_block(xp[1][1], qs_v, 1)
+    query_block(x, qr_v, 0)
     add_across(1)
-    query_block(x, qr_v, x)
     add_across(2)
     ff = add_across(3)
-    q_in.append(s.send(qs_v.at[1], qr_v.at[x], xp[1][0]))
 
     for copy in ff_in:
         s.landed(copy)
@@ -302,6 +308,16 @@
     s.landed(z_own[0])
     x_far = [(k, pass_on(piece(there, 0), xp[k - 1][0])) for k in (1, 3, 2)]
     cap_pair.append(pass_on(piece(there, 0), pair))
+    for to, v in xp + [(None, x)]:
+        for half in (0, 1):
+            g_in.append(
+                s.send(
+                    go.at[:, span(half * 4 + v, 256)],
+                    gs_v.at[span(x, 128), pl.ds(half * 256, 256)],
+                    to,
+                )
+            )
+
     z_far = []
     for k, copy in x_own:
         s.landed(copy)
@@ -321,7 +337,7 @@
     def _(i):
         rows = pl.ds(pl.multiple_of(i * 64, 64), 64)
         q = qr_v[0, rows, :].astype(F32) + qr_v[1, rows, :].astype(F32)
-        q = q + qr_v[2, rows, :].astype(F32) + qr_v[3, rows, :].astype(F32)
+        q = q + qr_v[2, rows, :].astype(F32)
         q_v[rows, :] = q.astype(BF)
 
     for copy in wkv_in:
@@ -339,15 +355,15 @@
         p = one[i]
         both = kv_v[0].astype(F32) * p + kv_v[1].astype(F32) * (1.0 - p)
         sel_v[i] = both.astype(BF)
-    kv_in = [s.send(sel_v.at[q // 2], kvr_v.at[mine], to) for to, q in quad_peers(*place)]
+    kv_over = s.send(sel_v.at[1 - zl], kvr_v.at[mine], across)
+    kv_pair = s.send(sel_v.at[zl], kvr_v.at[mine], pair)
     kvr_v[mine] = sel_v[zl]
-    for copy in g_in + kv_in:
+    for copy in g_in + [kv_pair]:
         s.landed(copy)
 
     inv_root = 1.0 / math.sqrt(HD)
 
-    @pl.loop(0, 4)
-    def _(h):
+    def attend(h):
         cols = pl.ds(pl.multiple_of(h * HD, HD), HD)
         q, g = q_v[:, cols], gs_v[:, cols]
         k, v = kvr_v[h, :, :HD], kvr_v[h, :, HD:]
@@ -365,6 +381,16 @@
         gv = lax.dot_general(probs_b, g, TN, preferred_element_type=F32)
         gkv_v[h, :, :HD] = gk.astype(BF)
         gkv_v[h, :, HD:] = gv.astype(BF)
+
+    @pl.loop(0, 2)
+    def _(i):
+        attend(zl * 2 + i)
+
+    s.landed(kv_over)
+    kv_far = s.send(kvr_v.at[theirs], kvr_v.at[theirs], pair)
+    attend(theirs)
+    s.landed(kv_far)
+    attend((1 - zl) * 2 + 1 - c)
 
     right, left = xp[0][0], xp[2][0]
 
@@ -522,7 +548,7 @@
             s.landed(copy)
             pass_on(out((y + 4 - k) % 4, zh).at[pl.ds(rows, rows)], zpair)
 
-    kv_over, kv_along = spread(kvp_v.at[here_dp], kv_at, 256)
+    dp_over, kv_along = spread(kvp_v.at[here_dp], kv_at, 256)
     for copy in r1_in + r2_in:
         s.landed(copy)
     for i in range(4):
@@ -541,7 +567,7 @@
         s.send(s1_v.at[(t % 2) * 2 + t // 2], t1_v.at[k], to) for k, (to, t) in enumerate(zp)
     ]
     t_in += [s.send(s2_v.at[v], t2_v.at[k], to) for k, (to, v) in enumerate(yp)]
-    pass_first(kv_over, kv_at, 256)
+    pass_first(dp_over, kv_at, 256)
     for copy in t_in:
         s.landed(copy)
     left, right = s1_v[at].astype(F32), s2_v[y].astype(F32)
@@ -567,7 +593,7 @@
     scratch = [
         (128, 4096), (128, 4096), (256, 2048), (4, 128, 4096), (32, 4096), (4096, 768), (384, 4096),
         (4096, 256), (1024, 2048), (512, 1024), (512, 512), None, (512, 384),
-        (256, 4096), (256, 4096), (256, 4096), (4, 32, 4096), (3, 32, 4096), (3, 512, 512), (4, 512, 512),
+        (256, 4096), (256, 4096), (256, 4096), (4, 32, 4096), (3, 32, 4096), (3, 512, 512), (2, 256, 512), (3, 512, 512),
         (512, 512), (2, 8, 32, 4096), (2, LCAP, 256), (2, LCAP, 256), (4, LCAP, 256),
         (512, 512), (512, 512), (4, LCAP, 256), (4, LCAP, 256), (512, 256), (8, 512, 256),
         (512, 2048), (4, 128, 2048), (3, 4, 32, 1024), (3, 128, 1024), (4, 32, 1024), (4, 32, 1024),

time: 187 us -> 182 us (0.973)
  Pallas kernels: 187 us -> 181 us
    pallas_call x1, Pallas kernels: 180 us -> 175 us  [main(): pl.pallas_call(kernel, out_shape=[jax.ShapeDtypeStruct(shape, BF) for sha...]
where the time goes in v6:
time: 182 us
  Pallas kernels  181 us (99%)
    pallas_call x1, Pallas kernels, main(): pl.pallas_call(kernel, out_shape=[jax.ShapeDtypeStruct(shape, BF) for sha...  175 us
    pallas_call x1, Pallas kernels, last(): pl.pallas_call(last_kernel, out_shape=[jax.ShapeDtypeStruct(shape, F32) f...  6.82 us

profile of v6, /device:TPU:0, one launch (start us, length us, event | category | flops | bytes accessed | tf_op | source)
XLA Modules:
  0.0 182.2 jit_solution(9312630925686398429)
XLA Ops:
  0.6 174.6 %main.1 = (bf16[128,2048]{1,0:T(8,128)(2,1)}, bf16[128,4096]{1,0:T(8,128)(2,1)}, bf16[8,32,2048]{2,1,0:T(8,128)(2,1)}, bf16[8,512,256]{2,1,0:T(8,128)(2,1)}) custom-call(bf16[128,4096]{1,0:T(8,128)(2,1)} %lat.3, bf16[128,2048]{1,0:T(8,128)(2,1)} %go.1, bf16[256,2048]{1,0:T(8,128)(2,1)} %wq.1, bf16[512,4096]{1,0:T(8,128)(2,1)} %ch.1, bf16[4096,384]{1,0:T(8,128)(2,1)} %wi0.1, ...), custom_call_target="tpu_custom_call" | custom-call | tf_op jit(solution)/shard_map/main/pallas_call | solution.py:603
  175.2 6.8 %last.1 = (f32[128,2048]{1,0:T(8,128)}, f32[128,4096]{1,0:T(8,128)}, f32[256,2048]{1,0:T(8,128)}, f32[4096,128]{1,0:T(8,128)}, f32[4096,128]{1,0:T(8,128)}) custom-call(bf16[128,2048]{1,0:T(8,128)(2,1)} %get-tuple-element.9.attn, bf16[128,4096]{1,0:T(8,128)(2,1)} %get-tuple-element.10.dxn, bf16[128,4096]{1,0:T(8,128)(2,1)} %lat.3, ...), custom_call_target="tpu_custom_call" | custom-call | tf_op jit(solution)/shard_map/last/pallas_call | solution.py:707

commit v7 on v6

--- a/solution.py
+++ b/solution.py
@@ -481,6 +481,56 @@
     qg_pair = s.send(ch_v.at[:, :, pl.ds(0, 2048)], grc_v, pair)
     q_grad(c, 2048)
 
+    s.landed(qg_pair)
+
+    @pl.loop(0, 32)
+    def _(i):
+        rows = pl.ds(pl.multiple_of((i % 8) * 16, 16), 16)
+        keep = ch_v[i // 8, rows, 2048:].astype(F32) + grc_v[i // 8, rows, :].astype(F32)
+        ch_v[i // 8, rows, 2048:] = keep.astype(BF)
+
+    r1_in = [
+        s.send(ch_v.at[:, span(v, 32), pl.ds(2048, 1024)], r1_v.at[k], to)
+        for k, (to, v) in enumerate(yp)
+    ]
+    r2_in = [
+        s.send(ch_v.at[(t % 2) * 2 + t // 2, :, pl.ds(3072, 1024)], r2_v.at[k], to)
+        for k, (to, t) in enumerate(zp)
+    ]
+
+    for copy in k2a_in + [k2b_in]:
+        s.landed(copy)
+    total = kvp_v[here_dp, first, :].astype(F32)
+    for k in range(3):
+        total = total + k2a_v[k].astype(F32)
+    kvp_v[here_dp, first, :] = total.astype(BF)
+    total = kvp_v[here_dp, second, :].astype(F32) + k2b_v[...].astype(F32)
+    kvp_v[here_dp, second, :] = total.astype(BF)
+
+    def kv_at(v, w):
+        return gkv_out.at[v * 2 + w]
+
+    def q_at(v, w):
+        return gq_out.at[w * 4 + v]
+
+    def spread(own, out, rows):
+        s.send(own, out(y, zh), None)
+        over = s.send(own.at[pl.ds(0, rows)], out(y, zh).at[pl.ds(0, rows)], zpair)
+        along = [(k, s.send(own, out(y, zh), yp[k - 1][0])) for k in (1, 3, 2)]
+        s.send(own.at[pl.ds(rows, rows)], out(y, zh).at[pl.ds(rows, rows)], zpair)
+        return over, along
+
+    def pass_first(over, out, rows):
+        s.landed(over)
+        for k in (1, 3, 2):
+            pass_on(out(y, 1 - zh).at[pl.ds(0, rows)], yp[k - 1][0])
+
+    def pass_second(along, out, rows):
+        for k, copy in along:
+            s.landed(copy)
+            pass_on(out((y + 4 - k) % 4, zh).at[pl.ds(rows, rows)], zpair)
+
+    dp_over, kv_along = spread(kvp_v.at[here_dp], kv_at, 256)
     @pl.loop(0, 4)
     def _(i):
         rows = pl.ds(pl.multiple_of(i * 256, 256), 256)
@@ -499,56 +549,6 @@
                 dxn_out.at[:, span(half * 4 + x, 512)],
                 to,
             )
-    s.landed(qg_pair)
-
-    @pl.loop(0, 32)
-    def _(i):
-        rows = pl.ds(pl.multiple_of((i % 8) * 16, 16), 16)
-        keep = ch_v[i // 8, rows, 2048:].astype(F32) + grc_v[i // 8, rows, :].astype(F32)
-        ch_v[i // 8, rows, 2048:] = keep.astype(BF)
-
-    r1_in = [
-        s.send(ch_v.at[:, span(v, 32), pl.ds(2048, 1024)], r1_v.at[k], to)
-        for k, (to, v) in enumerate(yp)
-    ]
-    r2_in = [
-        s.send(ch_v.at[(t % 2) * 2 + t // 2, :, pl.ds(3072, 1024)], r2_v.at[k], to)
-        for k, (to, t) in enumerate(zp)
-    ]
-
-    for copy in k2a_in + [k2b_in]:
-        s.landed(copy)
-    total = kvp_v[here_dp, first, :].astype(F32)
-    for k in range(3):
-        total = total + k2a_v[k].astype(F32)
-    kvp_v[here_dp, first, :] = total.astype(BF)
-    total = kvp_v[here_dp, second, :].astype(F32) + k2b_v[...].astype(F32)
-    kvp_v[here_dp, second, :] = total.astype(BF)
-
-    def kv_at(v, w):
-        return gkv_out.at[v * 2 + w]
-
-    def q_at(v, w):
-        return gq_out.at[w * 4 + v]
-
-    def spread(own, out, rows):
-        s.send(own, out(y, zh), None)
-        over = s.send(own.at[pl.ds(0, rows)], out(y, zh).at[pl.ds(0, rows)], zpair)
-        along = [(k, s.send(own, out(y, zh), yp[k - 1][0])) for k in (1, 3, 2)]
-        s.send(own.at[pl.ds(rows, rows)], out(y, zh).at[pl.ds(rows, rows)], zpair)
-        return over, along
-
-    def pass_first(over, out, rows):
-        s.landed(over)
-        for k in (1, 3, 2):
-            pass_on(out(y, 1 - zh).at[pl.ds(0, rows)], yp[k - 1][0])
-
-    def pass_second(along, out, rows):
-        for k, copy in along:
-            s.landed(copy)
-            pass_on(out((y + 4 - k) % 4, zh).at[pl.ds(rows, rows)], zpair)
-
-    dp_over, kv_along = spread(kvp_v.at[here_dp], kv_at, 256)
     for copy in r1_in + r2_in:
         s.landed(copy)
     for i in range(4):

time: 182 us -> 181 us (level); the launches traced: 182 us -> 178 us
  Pallas kernels: 181 us -> 178 us
    pallas_call x1, Pallas kernels: 175 us -> 171 us  [main(): pl.pallas_call(kernel, out_shape=[jax.ShapeDtypeStruct(shape, BF) for sha...]
where the time goes in v7:
time: 181 us; the launch traced here: 178 us
  Pallas kernels  178 us (98%)
    pallas_call x1, Pallas kernels, main(): pl.pallas_call(kernel, out_shape=[jax.ShapeDtypeStruct(shape, BF) for sha...  171 us
    pallas_call x1, Pallas kernels, last(): pl.pallas_call(last_kernel, out_shape=[jax.ShapeDtypeStruct(shape, F32) f...  6.82 us

profile of v7, /device:TPU:0, one launch (start us, length us, event | category | flops | bytes accessed | tf_op | source)
XLA Modules:
  0.0 178.4 jit_solution(5865625733361519075)
XLA Ops:
  0.6 170.8 %main.1 = (bf16[128,2048]{1,0:T(8,128)(2,1)}, bf16[128,4096]{1,0:T(8,128)(2,1)}, bf16[8,32,2048]{2,1,0:T(8,128)(2,1)}, bf16[8,512,256]{2,1,0:T(8,128)(2,1)}) custom-call(bf16[128,4096]{1,0:T(8,128)(2,1)} %lat.3, bf16[128,2048]{1,0:T(8,128)(2,1)} %go.1, bf16[256,2048]{1,0:T(8,128)(2,1)} %wq.1, bf16[512,4096]{1,0:T(8,128)(2,1)} %ch.1, bf16[4096,384]{1,0:T(8,128)(2,1)} %wi0.1, ...), custom_call_target="tpu_custom_call" | custom-call | tf_op jit(solution)/shard_map/main/pallas_call | solution.py:603
  171.4 6.8 %last.1 = (f32[128,2048]{1,0:T(8,128)}, f32[128,4096]{1,0:T(8,128)}, f32[256,2048]{1,0:T(8,128)}, f32[4096,128]{1,0:T(8,128)}, f32[4096,128]{1,0:T(8,128)}) custom-call(bf16[128,2048]{1,0:T(8,128)(2,1)} %get-tuple-element.9.attn, bf16[128,4096]{1,0:T(8,128)(2,1)} %get-tuple-element.10.dxn, bf16[128,4096]{1,0:T(8,128)(2,1)} %lat.3, ...), custom_call_target="tpu_custom_call" | custom-call | tf_op jit(solution)/shard_map/last/pallas_call | solution.py:707
